TPU v7x, 32 devices: a whole 2x2x4 slice. The times are simulated.
32 devices in a mesh: leaf: 8 (over z, y), front: 4 (over x, core).
Axes of the slice: x: 2, y: 2, z: 4, core: 2. Of those that a mesh axis runs over, the one named last changes fastest.
Arguments:
- right_side: bfloat16 [32, 40960], P(None, ('leaf', 'front')), may hold values from -6 to 6
- send_order: int32 [40960], P(('leaf', 'front')), may hold values from 0 to 1279, as said below
- owner_order: int32 [40960], P(('leaf', 'front')), may hold values from 0 to 1279, as said below
- live_rows: int32 [7], replicated, may hold values from 2048 to 4096, as said below
- lower_leaf: bfloat16 [1536, 12288], P(None, ('leaf', 'front')), may hold values from -0.109375 to 0.109375
- upper_leaf: bfloat16 [1536, 12288], P(None, ('leaf', 'front')), may hold values from -0.109375 to 0.109375
- lower_first: bfloat16 [4096, 16384], P(None, ('leaf', 'front')), may hold values from -0.0625 to 0.0625
- lower_second: bfloat16 [4096, 8192], P(None, ('leaf', 'front')), may hold values from -0.0625 to 0.0625
- lower_third: bfloat16 [4096, 4096], P(None, ('leaf', 'front')), may hold values from -0.0625 to 0.0625
- upper_first: bfloat16 [4096, 16384], P(None, ('leaf', 'front')), may hold values from -0.0625 to 0.0625
- upper_second: bfloat16 [4096, 8192], P(None, ('leaf', 'front')), may hold values from -0.0625 to 0.0625
- upper_third: bfloat16 [4096, 4096], P(None, ('leaf', 'front')), may hold values from -0.0625 to 0.0625
- downlink_first: bfloat16 [4096, 12288], P(None, ('leaf', 'front')), may hold values from -0.21875 to 0.21875
- downlink_second: bfloat16 [4096, 16384], P(None, ('leaf', 'front')), may hold values from -0.125 to 0.125
- downlink_third: bfloat16 [4096, 8192], P(None, ('leaf', 'front')), may hold values from -0.125 to 0.125
- uplink_first: bfloat16 [4096, 12288], P(None, ('leaf', 'front')), may hold values from -0.0625 to 0.0625
- uplink_second: bfloat16 [4096, 16384], P(None, ('leaf', 'front')), may hold values from -0.0625 to 0.0625
- uplink_third: bfloat16 [4096, 8192], P(None, ('leaf', 'front')), may hold values from -0.0625 to 0.0625
- pattern_first: int32 [64, 192], P(None, ('leaf', 'front')), may hold values 0 or 1
- pattern_second: int32 [64, 256], P(None, ('leaf', 'front')), may hold values 0 or 1
- pattern_third: int32 [64, 128], P(None, ('leaf', 'front')), may hold values 0 or 1
Outputs:
- solution: bfloat16 [32, 40960], P(None, ('leaf', 'front'))
Inputs may be any that keep to these rules, and one draw needn't show every extreme that they name: `send_order`: each device's 1280 entries are a permutation of 0 to 1279. `owner_order`: each device's 1280 entries are a permutation of 0 to 1279. `live_rows`: multiples of 64.
All inputs are finite; a program needn't handle non-finite values. No bound on the sum of `pattern_first` or of `pattern_second` or of `pattern_third` on one device may be relied on, other than what follows from the above.
Results may differ from a plain program's by a relative error of at most 0.023.
Values may be sent and summed in bfloat16 or wider, within the bound.
A program may use at most 128 MiB of HBM per device.

v0:
```python
import jax
import jax.numpy as jnp
from jax import lax
from jax.sharding import PartitionSpec as P


def partner_2(value, axis, distance):
    mask = 2**distance
    pairs = [(source, source ^ mask) for source in range(lax.axis_size(axis))]
    return lax.ppermute(value, axis, pairs)


def spread(pattern, block):
    wide = jnp.repeat(pattern, block, axis=0)
    return jnp.repeat(wide, block, axis=1).astype(jnp.bfloat16)


def collect_group(portion, level, place):
    gathered = lax.all_gather(portion, "front", axis=1, tiled=True)
    for level_bit in range(level):
        partner = partner_2(gathered, "leaf", level_bit)
        upper_side = place >> level_bit & 1 == 1
        gathered = jnp.where(
            upper_side,
            jnp.concatenate([partner, gathered], axis=1),
            jnp.concatenate([gathered, partner], axis=1),
        )
    return gathered


def leaf_term(portion, matrix):
    return jnp.dot(portion, matrix, preferred_element_type=jnp.float32)


def per_device(
    right_side,
    send_order,
    owner_order,
    live_rows,
    lower_leaf,
    upper_leaf,
    lower_first,
    lower_second,
    lower_third,
    upper_first,
    upper_second,
    upper_third,
    downlink_first,
    downlink_second,
    downlink_third,
    uplink_first,
    uplink_second,
    uplink_third,
    pattern_first,
    pattern_second,
    pattern_third,
):
    fronts = lax.axis_size("front")
    leaves = lax.axis_size("leaf")
    place = lax.axis_index("leaf")
    column = lax.axis_index("front")
    columns = right_side.shape[0]
    leaf_rows = lower_leaf.shape[1]
    sep = lower_first.shape[0]
    lowers = [lower_first, lower_second, lower_third]
    uppers = [upper_first, upper_second, upper_third]
    downs = [downlink_first, downlink_second, downlink_third]
    backs = [uplink_first, uplink_second, uplink_third]
    patterns = [pattern_first, pattern_second, pattern_third]
    block = downlink_first.shape[0] // pattern_first.shape[0]
    pieces = [lower_first.shape[1], lower_second.shape[1], lower_third.shape[1]]
    starts = [0, leaves // 2, leaves // 2 + leaves // 4]
    outgoing = jnp.take(right_side, send_order, axis=1)
    arrived = lax.all_to_all(outgoing, ("leaf", "front"), split_axis=1, concat_axis=1, tiled=True)
    ordered = jnp.take(arrived, owner_order, axis=1)
    leaf_rhs = ordered[:, :leaf_rows]
    level_rhs = []
    offset = leaf_rows
    for level in range(1, 4):
        level_rhs.append(ordered[:, offset : offset + pieces[level - 1]])
        offset = offset + pieces[level - 1]
    piece_masks = []
    full_masks = []
    within = []
    for level in range(1, 4):
        group = 2**level
        member = place & group - 1
        node_live = lax.dynamic_index_in_dim(
            live_rows, starts[level - 1] + (place >> level), 0, keepdims=False
        )
        first_row = (member * fronts + column) * pieces[level - 1]
        piece_masks.append(
            (first_row + jnp.arange(pieces[level - 1], dtype=jnp.int32) < node_live).astype(
                jnp.float32
            )[None, :]
        )
        full_masks.append(
            (jnp.arange(sep, dtype=jnp.int32) < node_live).astype(jnp.float32)[None, :]
        )
        within.append(member)
    expanded = [spread(patterns[index], block) for index in range(3)]
    leaf_y = leaf_term(
        lax.all_gather(leaf_rhs, "front", axis=1, tiled=True), matrix=lower_leaf
    ).astype(jnp.bfloat16)
    children = leaf_y
    level_y = []
    for level in range(1, 4):
        group = 2**level
        piece = pieces[level - 1]
        member = within[level - 1]
        link = downs[level - 1] * expanded[level - 1]
        own_rhs = level_rhs[level - 1].astype(jnp.float32)
        shaped = link.reshape(group, fronts, piece, link.shape[1])
        term = jnp.einsum(
            "kc,jfpc->kfjp", children, shaped, preferred_element_type=jnp.float32
        ).reshape(columns, sep)
        first_row = (column * group + member) * piece
        current = lax.dynamic_slice_in_dim(term, first_row, piece, 1)
        term = lax.dynamic_update_slice_in_dim(term, current - own_rhs, first_row, 1)
        share = lax.psum_scatter(
            term.astype(jnp.bfloat16), "front", scatter_dimension=1, tiled=True
        ).astype(jnp.float32)
        for level_bit in reversed(range(level)):
            middle = share.shape[1] // 2
            lower_half = share[:, :middle]
            upper_half = share[:, middle:]
            high_side = place >> level_bit & 1 == 1
            keeping = jnp.where(high_side, upper_half, lower_half)
            sending = jnp.where(high_side, lower_half, upper_half)
            share = keeping + partner_2(sending.astype(jnp.bfloat16), "leaf", level_bit).astype(
                sending.dtype
            )
        reduced_piece = (-share * piece_masks[level - 1]).astype(jnp.bfloat16)
        reduced_full = collect_group(reduced_piece, level, place)
        solved = jnp.dot(reduced_full, lowers[level - 1], preferred_element_type=jnp.float32)
        found = (solved * piece_masks[level - 1]).astype(jnp.bfloat16)
        level_y.append(found)
        children = found
    level_x = [None, None, None]
    top_full = collect_group(level_y[2], 3, place)
    level_x[2] = (
        jnp.dot(top_full, upper_third, preferred_element_type=jnp.float32) * piece_masks[2]
    ).astype(jnp.bfloat16)
    for level in (2, 1):
        back = backs[level] * expanded[level]
        parent_full = collect_group(level_x[level], level + 1, place)
        update = level_y[level - 1].astype(jnp.float32) - jnp.dot(
            parent_full, back, preferred_element_type=jnp.float32
        )
        reduced = (update * piece_masks[level - 1]).astype(jnp.bfloat16)
        reduced_full = collect_group(reduced, level, place)
        solved = jnp.dot(reduced_full, uppers[level - 1], preferred_element_type=jnp.float32)
        level_x[level - 1] = (solved * piece_masks[level - 1]).astype(jnp.bfloat16)
    back = uplink_first * expanded[0]
    parent_full = collect_group(level_x[0], 1, place)
    update = (
        leaf_y.astype(jnp.float32) - jnp.dot(parent_full, back, preferred_element_type=jnp.float32)
    ).astype(jnp.bfloat16)
    leaf_x = leaf_term(
        lax.all_gather(update, "front", axis=1, tiled=True), matrix=upper_leaf
    ).astype(jnp.bfloat16)
    placed = jnp.concatenate([leaf_x, level_x[0], level_x[1], level_x[2]], axis=1)
    outbound = jnp.zeros_like(placed).at[:, owner_order].set(placed)
    returned = lax.all_to_all(outbound, ("leaf", "front"), split_axis=1, concat_axis=1, tiled=True)
    return jnp.zeros_like(returned).at[:, send_order].set(returned)


def solution(mesh):
    placed = (
        P(None, ("leaf", "front")),
        P(("leaf", "front")),
        P(("leaf", "front")),
        P(),
        P(None, ("leaf", "front")),
        P(None, ("leaf", "front")),
        P(None, ("leaf", "front")),
        P(None, ("leaf", "front")),
        P(None, ("leaf", "front")),
        P(None, ("leaf", "front")),
        P(None, ("leaf", "front")),
        P(None, ("leaf", "front")),
        P(None, ("leaf", "front")),
        P(None, ("leaf", "front")),
        P(None, ("leaf", "front")),
        P(None, ("leaf", "front")),
        P(None, ("leaf", "front")),
        P(None, ("leaf", "front")),
        P(None, ("leaf", "front")),
        P(None, ("leaf", "front")),
        P(None, ("leaf", "front")),
    )
    return jax.shard_map(
        per_device,
        mesh=mesh,
        in_specs=placed,
        out_specs=P(None, ("leaf", "front")),
        check_vma=False,
    )
```

profile of v0, /device:TPU:0, one launch (start us, length us, event | category | flops | bytes accessed | tf_op | source)
XLA Modules:
  0.0 378.0 jit_solution(1954302768207969108)
XLA Ops:
  9.2 2.8 gather_fusion
  13.5 7.3 %all-to-all-start = ((bf16[32,2,640]{2,1,0:T(2,128)(2,1)}), bf16[32,2,640]{2,1,0:T(2,128)(2,1)S(1)}, u32[]{:S(2)}, u32[]{:S(2)}) async-start(bf16[32,2,640]{2,1,0:T(2,128)(2,1)} %reshape.110), calls=%async_computation | async-start | bytes 163840 | tf_op jit(solution)/shard_map/all_to_all | solution.py:74
  22.2 4.7 %copy.70 = bf16[4096,384]{0,1:T(8,128)(2,1)} copy(bf16[4096,384]{1,0:T(8,128)(2,1)} %param.35) | data formatting | bytes 6291456 | tf_op args[12]
  26.9 4.8 %copy.81 = bf16[4096,384]{0,1:T(8,128)(2,1)} copy(bf16[4096,384]{1,0:T(8,128)(2,1)} %param.38) | data formatting | bytes 6291456 | tf_op args[15]
  31.9 5.9 %bitcast_multiply_fusion.2 = (bf16[4096,384]{0,1:T(8,128)(2,1)}, bf16[4096,384]{0,1:T(8,128)(2,1)}) fusion(bf16[4096,384]{0,1:T(8,128)(2,1)} %copy.81, bf16[4096,6]{0,1:T(8,128)(2,1)S(1)} %convert_element_type.171, bf16[4096,384]{0,1:T(8,128)(2,1)} %copy.70), kind=kLoop, calls=%fused_computation.6 | loop fusion | flops 3145728 | bytes 12632064 | tf_op jit(solution)/shard_map/mul | solution.py:154
  37.8 4.6 %copy.90 = bf16[4096,384]{1,0:T(8,128)(2,1)} copy(bf16[4096,384]{0,1:T(8,128)(2,1)} %get-tuple-element.7) | data formatting | bytes 6291456 | tf_op jit(solution)/shard_map/reshape | solution.py:113
  43.1 2.8 gather_fusion.1
  46.1 5.3 %all_gather.33 = bf16[32,1536]{1,0:T(8,128)(2,1)S(1)} all-gather(bf16[32,384]{1,0:T(8,128)(2,1)S(1)} %slice.68), channel_id=1, replica_groups=mesh['leaf'=8,'front'=4] {'front'}, dimensions={1}, use_global_device_ids=true | all-gather | bytes 122880 | tf_op jit(solution)/shard_map/all_gather | solution.py:103
  51.5 1.5 convolution_convert_fusion.1
  53.0 3.0 convolution_bitcast_fusion.2
  58.4 20.8 %reduce-scatter.4.cloned.1.call-done = bf16[32,1024]{1,0:T(8,128)(2,1)} async-done(((bf16[32,4096]{1,0:T(8,128)(2,1)}), bf16[32,1024]{1,0:T(8,128)(2,1)}) %reduce-scatter.4.cloned.1.call-update) | async-done | bytes 65552 | tf_op jit(solution)/shard_map/reduce_scatter | solution.py:120
  82.2 1.8 collective-permute-done
  84.0 5.4 %all_gather.34 = bf16[32,2048]{1,0:T(8,128)(2,1)S(1)} all-gather(bf16[32,512]{1,0:T(8,128)(2,1)S(1)} %multiply_convert_fusion), channel_id=1, replica_groups=mesh['leaf'=8,'front'=4] {'front'}, dimensions={1}, use_global_device_ids=true | all-gather | bytes 163840 | tf_op jit(solution)/shard_map/all_gather | solution.py:19
  90.9 6.4 %copy.73 = bf16[4096,512]{0,1:T(8,128)(2,1)} copy(bf16[4096,512]{1,0:T(8,128)(2,1)} %param.36) | data formatting | bytes 8388608 | tf_op args[13]
  97.3 6.4 %copy.80 = bf16[4096,512]{0,1:T(8,128)(2,1)} copy(bf16[4096,512]{1,0:T(8,128)(2,1)} %param.39) | data formatting | bytes 8388608 | tf_op args[16]
  104.0 7.3 %bitcast_multiply_fusion = (bf16[4096,512]{0,1:T(8,128)(2,1)}, bf16[4096,512]{0,1:T(8,128)(2,1)}) fusion(bf16[4096,512]{0,1:T(8,128)(2,1)} %copy.80, bf16[4096,8]{0,1:T(8,128)(2,1)S(1)} %convert_element_type.183, bf16[4096,512]{0,1:T(8,128)(2,1)} %copy.73), kind=kLoop, calls=%fused_computation.4 | loop fusion | flops 4194304 | bytes 16842752 | tf_op jit(solution)/shard_map/mul | solution.py:145
  111.3 6.5 %copy.91 = bf16[4096,512]{1,0:T(8,128)(2,1)} copy(bf16[4096,512]{0,1:T(8,128)(2,1)} %get-tuple-element.9) | data formatting | bytes 8388608 | tf_op jit(solution)/shard_map/reshape | solution.py:113
  117.8 3.1 fusion.2
  124.0 19.2 %reduce-scatter.6.cloned.1.call-done = bf16[32,1024]{1,0:T(8,128)(2,1)} async-done(((bf16[32,4096]{1,0:T(8,128)(2,1)}), bf16[32,1024]{1,0:T(8,128)(2,1)}) %reduce-scatter.6.cloned.1.call-update) | async-done | bytes 65552 | tf_op jit(solution)/shard_map/reduce_scatter | solution.py:120
  144.2 1.6 collective-permute-start.2
  145.7 2.4 collective-permute-done.2
  148.2 1.5 collective-permute-start.3
  150.3 1.7 collective-permute-done.3
  152.0 5.4 %all_gather.35 = bf16[32,1024]{1,0:T(8,128)(2,1)S(1)} all-gather(bf16[32,256]{1,0:T(8,128)(2,1)S(1)} %multiply_convert_fusion.1), channel_id=1, replica_groups=mesh['leaf'=8,'front'=4] {'front'}, dimensions={1}, use_global_device_ids=true | all-gather | bytes 81920 | tf_op jit(solution)/shard_map/all_gather | solution.py:19
  158.9 2.9 collective-permute-done.4
  161.8 1.6 collective-permute-start.5
  163.3 4.2 %copy.76 = bf16[4096,256]{0,1:T(8,128)(2,1)} copy(bf16[4096,256]{1,0:T(8,128)(2,1)} %param.37) | data formatting | bytes 4194304 | tf_op args[14]
  167.5 4.1 %copy.79 = bf16[4096,256]{0,1:T(8,128)(2,1)} copy(bf16[4096,256]{1,0:T(8,128)(2,1)} %param.40) | data formatting | bytes 4194304 | tf_op args[17]
  171.8 4.6 %bitcast_multiply_fusion.4 = (bf16[4096,256]{0,1:T(8,128)(2,1)}, bf16[4096,256]{0,1:T(8,128)(2,1)}) fusion(bf16[4096,256]{0,1:T(8,128)(2,1)} %copy.79, bf16[4096,4]{0,1:T(4,128)(2,1)S(1)} %convert_element_type.197, bf16[4096,256]{0,1:T(8,128)(2,1)} %copy.76), kind=kLoop, calls=%fused_computation.8 | loop fusion | flops 2097152 | bytes 8421376 | tf_op jit(solution)/shard_map/mul | solution.py:145
  176.4 4.1 %copy.92 = bf16[4096,256]{1,0:T(8,128)(2,1)} copy(bf16[4096,256]{0,1:T(8,128)(2,1)} %get-tuple-element.11) | data formatting | bytes 4194304 | tf_op jit(solution)/shard_map/reshape | solution.py:113
  181.0 2.3 convolution_bitcast_fusion
  184.7 19.3 %reduce-scatter.8.cloned.1.call-done = bf16[32,1024]{1,0:T(8,128)(2,1)} async-done(((bf16[32,4096]{1,0:T(8,128)(2,1)}), bf16[32,1024]{1,0:T(8,128)(2,1)}) %reduce-scatter.8.cloned.1.call-update) | async-done | bytes 65552 | tf_op jit(solution)/shard_map/reduce_scatter | solution.py:120
  204.9 2.5 collective-permute-start.6
  207.3 2.5 collective-permute-done.6
  211.3 2.3 collective-permute-done.7
  215.8 1.5 collective-permute-done.8
  217.4 5.2 %all_gather.36 = bf16[32,512]{1,0:T(8,128)(2,1)S(1)} all-gather(bf16[32,128]{1,0:T(8,128)(2,1)S(1)} %multiply_convert_fusion.2), channel_id=1, replica_groups=mesh['leaf'=8,'front'=4] {'front'}, dimensions={1}, use_global_device_ids=true | all-gather | bytes 40960 | tf_op jit(solution)/shard_map/all_gather | solution.py:19
  224.0 2.5 collective-permute-done.9
  228.0 2.9 collective-permute-done.10
  230.9 2.4 collective-permute-start.11
  233.3 4.9 %collective-permute-done.11 = bf16[32,2048]{1,0:T(8,128)(2,1)S(1)} collective-permute-done((bf16[32,2048]{1,0:T(8,128)(2,1)S(1)}, bf16[32,2048]{1,0:T(8,128)(2,1)S(1)}, u32[]{:S(2)}, u32[]{:S(2)}) %collective-permute-start.11) | collective-permute-done | bytes 131104 | tf_op jit(solution)/shard_map/ppermute | solution.py:10
  239.7 5.2 %all_gather.37 = bf16[32,512]{1,0:T(8,128)(2,1)S(1)} all-gather(bf16[32,128]{1,0:T(8,128)(2,1)S(1)} %fusion.9), channel_id=1, replica_groups=mesh['leaf'=8,'front'=4] {'front'}, dimensions={1}, use_global_device_ids=true | all-gather | bytes 40960 | tf_op jit(solution)/shard_map/all_gather | solution.py:19
  246.4 2.5 collective-permute-done.12
  249.4 3.8 %collective-permute-done.13 = bf16[32,1024]{1,0:T(8,128)(2,1)S(1)} collective-permute-done((bf16[32,1024]{1,0:T(8,128)(2,1)S(1)}, bf16[32,1024]{1,0:T(8,128)(2,1)S(1)}, u32[]{:S(2)}, u32[]{:S(2)}) %collective-permute-start.13) | collective-permute-done | bytes 65568 | tf_op jit(solution)/shard_map/ppermute | solution.py:10
  253.2 1.9 collective-permute-start.14
  255.1 5.5 %collective-permute-done.14 = bf16[32,2048]{1,0:T(8,128)(2,1)S(1)} collective-permute-done((bf16[32,2048]{1,0:T(8,128)(2,1)S(1)}, bf16[32,2048]{1,0:T(8,128)(2,1)S(1)}, u32[]{:S(2)}, u32[]{:S(2)}) %collective-permute-start.14) | collective-permute-done | bytes 131104 | tf_op jit(solution)/shard_map/ppermute | solution.py:10
  262.1 5.3 %all_gather.38 = bf16[32,512]{1,0:T(8,128)(2,1)S(1)} all-gather(bf16[32,128]{1,0:T(8,128)(2,1)S(1)} %fusion.10), channel_id=1, replica_groups=mesh['leaf'=8,'front'=4] {'front'}, dimensions={1}, use_global_device_ids=true | all-gather | bytes 40960 | tf_op jit(solution)/shard_map/all_gather | solution.py:19
  268.8 2.5 collective-permute-done.15
  271.4 4.2 %collective-permute-done.16 = bf16[32,1024]{1,0:T(8,128)(2,1)S(1)} collective-permute-done((bf16[32,1024]{1,0:T(8,128)(2,1)S(1)}, bf16[32,1024]{1,0:T(8,128)(2,1)S(1)}, u32[]{:S(2)}, u32[]{:S(2)}) %collective-permute-start.16) | collective-permute-done | bytes 65568 | tf_op jit(solution)/shard_map/ppermute | solution.py:10
  277.2 5.8 %collective-permute-done.17 = bf16[32,2048]{1,0:T(8,128)(2,1)S(1)} collective-permute-done((bf16[32,2048]{1,0:T(8,128)(2,1)S(1)}, bf16[32,2048]{1,0:T(8,128)(2,1)S(1)}, u32[]{:S(2)}, u32[]{:S(2)}) %collective-permute-start.17) | collective-permute-done | bytes 131104 | tf_op jit(solution)/shard_map/ppermute | solution.py:10
  283.7 5.2 %all_gather.39 = bf16[32,1024]{1,0:T(8,128)(2,1)S(1)} all-gather(bf16[32,256]{1,0:T(8,128)(2,1)S(1)} %fusion.7), channel_id=1, replica_groups=mesh['leaf'=8,'front'=4] {'front'}, dimensions={1}, use_global_device_ids=true | all-gather | bytes 81920 | tf_op jit(solution)/shard_map/all_gather | solution.py:19
  290.4 2.9 collective-permute-done.18
  293.4 5.0 %collective-permute-done.19 = bf16[32,2048]{1,0:T(8,128)(2,1)S(1)} collective-permute-done((bf16[32,2048]{1,0:T(8,128)(2,1)S(1)}, bf16[32,2048]{1,0:T(8,128)(2,1)S(1)}, u32[]{:S(2)}, u32[]{:S(2)}) %collective-permute-start.19) | collective-permute-done | bytes 131104 | tf_op jit(solution)/shard_map/ppermute | solution.py:10
  298.8 5.2 %all_gather.40 = bf16[32,1024]{1,0:T(8,128)(2,1)S(1)} all-gather(bf16[32,256]{1,0:T(8,128)(2,1)S(1)} %fusion.8), channel_id=1, replica_groups=mesh['leaf'=8,'front'=4] {'front'}, dimensions={1}, use_global_device_ids=true | all-gather | bytes 81920 | tf_op jit(solution)/shard_map/all_gather | solution.py:19
  305.5 2.9 collective-permute-done.20
  308.7 4.7 %collective-permute-done.21 = bf16[32,2048]{1,0:T(8,128)(2,1)S(1)} collective-permute-done((bf16[32,2048]{1,0:T(8,128)(2,1)S(1)}, bf16[32,2048]{1,0:T(8,128)(2,1)S(1)}, u32[]{:S(2)}, u32[]{:S(2)}) %collective-permute-start.21) | collective-permute-done | bytes 131104 | tf_op jit(solution)/shard_map/ppermute | solution.py:10
  314.8 5.6 %all_gather.41 = bf16[32,2048]{1,0:T(8,128)(2,1)S(1)} all-gather(bf16[32,512]{1,0:T(8,128)(2,1)S(1)} %fusion.1), channel_id=1, replica_groups=mesh['leaf'=8,'front'=4] {'front'}, dimensions={1}, use_global_device_ids=true | all-gather | bytes 163840 | tf_op jit(solution)/shard_map/all_gather | solution.py:19
  321.8 4.3 %collective-permute-done.22 = bf16[32,2048]{1,0:T(8,128)(2,1)S(1)} collective-permute-done((bf16[32,2048]{1,0:T(8,128)(2,1)S(1)}, bf16[32,2048]{1,0:T(8,128)(2,1)S(1)}, u32[]{:S(2)}, u32[]{:S(2)}) %collective-permute-start.22) | collective-permute-done | bytes 131104 | tf_op jit(solution)/shard_map/ppermute | solution.py:10
  326.9 5.4 %all_gather.42 = bf16[32,2048]{1,0:T(8,128)(2,1)S(1)} all-gather(bf16[32,512]{1,0:T(8,128)(2,1)S(1)} %fusion.3), channel_id=1, replica_groups=mesh['leaf'=8,'front'=4] {'front'}, dimensions={1}, use_global_device_ids=true | all-gather | bytes 163840 | tf_op jit(solution)/shard_map/all_gather | solution.py:19
  333.8 4.3 %collective-permute-done.23 = bf16[32,2048]{1,0:T(8,128)(2,1)S(1)} collective-permute-done((bf16[32,2048]{1,0:T(8,128)(2,1)S(1)}, bf16[32,2048]{1,0:T(8,128)(2,1)S(1)}, u32[]{:S(2)}, u32[]{:S(2)}) %collective-permute-start.23) | collective-permute-done | bytes 131104 | tf_op jit(solution)/shard_map/ppermute | solution.py:10
  339.1 5.6 %all_gather.43 = bf16[32,1536]{1,0:T(8,128)(2,1)S(1)} all-gather(bf16[32,384]{1,0:T(8,128)(2,1)S(1)} %fusion.4), channel_id=1, replica_groups=mesh['leaf'=8,'front'=4] {'front'}, dimensions={1}, use_global_device_ids=true | all-gather | bytes 122880 | tf_op jit(solution)/shard_map/all_gather | solution.py:160
  345.2 6.3 %scatter_custom_fusion = bf16[32,1280]{0,1:T(8,128)(2,1)S(1)} fusion(s32[1280]{0:T(1024)S(1)} %compare_select_fusion, bf16[1280,32]{1,0:T(8,128)(2,1)S(1)} %copy.82, bf16[]{:T(256)} %constant.15.clone.1), kind=kCustom, calls=%fused_computation.102 | custom fusion | bytes 81922 | tf_op jit(solution)/shard_map/scatter | solution.py:163
  352.1 11.2 %all_to_all.24 = bf16[32,2,640]{2,1,0:T(2,128)(2,1)S(1)} all-to-all(bf16[32,2,640]{2,1,0:T(2,128)(2,1)S(1)} %reshape.112), channel_id=1, replica_groups=mesh['leaf'=8,'front'=4] {'leaf','front'}, dimensions={0} | all-to-all | bytes 163840 | tf_op jit(solution)/shard_map/all_to_all | solution.py:164
  364.3 6.3 %scatter_custom_fusion.1 = bf16[32,1280]{0,1:T(8,128)(2,1)S(1)} fusion(s32[1280]{0:T(1024)S(1)} %compare_select_fusion.1, bf16[1280,32]{1,0:T(8,128)(2,1)S(1)} %copy.85, bf16[]{:T(256)} %constant.15.clone.1), kind=kCustom, calls=%fused_computation.100 | custom fusion | bytes 81922 | tf_op jit(solution)/shard_map/scatter | solution.py:165
  (134 shorter events, 51.0 us)
Async XLA Ops:
  6.5 174.0 %copy-start = (bf16[4096,256]{1,0:T(8,128)(2,1)S(1)}, bf16[4096,256]{1,0:T(8,128)(2,1)}, u32[]{:S(2)}) copy-start(bf16[4096,256]{1,0:T(8,128)(2,1)} %param.30) | copy-start | bytes 6291460
  13.5 29.0 %all-to-all-start = ((bf16[32,2,640]{2,1,0:T(2,128)(2,1)}), bf16[32,2,640]{2,1,0:T(2,128)(2,1)S(1)}, u32[]{:S(2)}, u32[]{:S(2)}) async-start(bf16[32,2,640]{2,1,0:T(2,128)(2,1)} %reshape.110), calls=%async_computation | async-start | bytes 163840 | tf_op jit(solution)/shard_map/all_to_all | solution.py:74
  20.8 58.3 %reduce-scatter.4.cloned.1.call-start = ((), (), s32[]{:S(2)}) async-start(), calls=%async_computation.5 | async-start | bytes 327680 | tf_op jit(solution)/shard_map/reduce_scatter | solution.py:120
  26.9 4.8 %copy-start.9 = (s32[64,6]{0,1:T(8,128)S(1)}, s32[64,6]{0,1:T(8,128)}, u32[]{:S(2)}) copy-start(s32[64,6]{0,1:T(8,128)} %param.41) | copy-start | bytes 4612
  53.0 4.7 %copy-start.8 = (s32[7]{0:T(128)S(1)}, s32[7]{0:T(128)}, u32[]{:S(2)}) copy-start(s32[7]{0:T(128)} %param.26) | copy-start | bytes 88
  57.7 85.6 %reduce-scatter.6.cloned.1.call-start = ((), (), s32[]{:S(2)}) async-start(), calls=%async_computation.6 | async-start | bytes 327680 | tf_op jit(solution)/shard_map/reduce_scatter | solution.py:120
  80.0 4.0 %collective-permute-start = (bf16[32,512]{1,0:T(8,128)(2,1)S(1)}, bf16[32,512]{1,0:T(8,128)(2,1)S(1)}, u32[]{:S(2)}, u32[]{:S(2)}) collective-permute-start(bf16[32,512]{1,0:T(8,128)(2,1)S(1)} %select_convert_fusion.2), channel_id=1, source_target_pairs={{0,4},{4,0},{8,12},{12,8},{16,20},{20,16},{24,28},{28,24},{1,5},{5... | collective-permute-start | bytes 98312 | tf_op jit(solution)/shard_map/ppermute | solution.py:10
  89.4 28.4 %collective-permute-start.1 = (bf16[32,2048]{1,0:T(8,128)(2,1)S(1)}, bf16[32,2048]{1,0:T(8,128)(2,1)S(1)}, u32[]{:S(2)}, u32[]{:S(2)}) collective-permute-start(bf16[32,2048]{1,0:T(8,128)(2,1)S(1)} %all_gather.34), channel_id=1, source_target_pairs={{0,4},{4,0},{8,12},{12,8},{16,20},{20,16},{24,28},{28,24},{1,5},{5... | collective-permute-start | bytes 393224 | tf_op jit(solution)/shard_map/ppermute | solution.py:10
  97.3 6.4 %copy-start.10 = (s32[64,8]{0,1:T(8,128)S(1)}, s32[64,8]{0,1:T(8,128)}, u32[]{:S(2)}) copy-start(s32[64,8]{0,1:T(8,128)} %param.42) | copy-start | bytes 6148
  117.8 3.4 copy-start.1
  124.0 80.0 %reduce-scatter.8.cloned.1.call-start = ((), (), s32[]{:S(2)}) async-start(), calls=%async_computation.7 | async-start | bytes 327680 | tf_op jit(solution)/shard_map/reduce_scatter | solution.py:120
  144.2 4.0 %collective-permute-start.2 = (bf16[32,512]{1,0:T(8,128)(2,1)S(1)}, bf16[32,512]{1,0:T(8,128)(2,1)S(1)}, u32[]{:S(2)}, u32[]{:S(2)}) collective-permute-start(bf16[32,512]{1,0:T(8,128)(2,1)S(1)} %select_convert_fusion.1), channel_id=1, source_target_pairs={{0,8},{4,12},{8,0},{12,4},{16,24},{20,28},{24,16},{28,20},{1,9},{5... | collective-permute-start | bytes 98312 | tf_op jit(solution)/shard_map/ppermute | solution.py:10
  148.2 3.8 %collective-permute-start.3 = (bf16[32,256]{1,0:T(8,128)(2,1)S(1)}, bf16[32,256]{1,0:T(8,128)(2,1)S(1)}, u32[]{:S(2)}, u32[]{:S(2)}) collective-permute-start(bf16[32,256]{1,0:T(8,128)(2,1)S(1)} %select_convert_fusion.4), channel_id=1, source_target_pairs={{0,4},{4,0},{8,12},{12,8},{16,20},{20,16},{24,28},{28,24},{1,5},{5... | collective-permute-start | bytes 49160 | tf_op jit(solution)/shard_map/ppermute | solution.py:10
  157.4 4.3 %collective-permute-start.4 = (bf16[32,1024]{1,0:T(8,128)(2,1)S(1)}, bf16[32,1024]{1,0:T(8,128)(2,1)S(1)}, u32[]{:S(2)}, u32[]{:S(2)}) collective-permute-start(bf16[32,1024]{1,0:T(8,128)(2,1)S(1)} %all_gather.35), channel_id=1, source_target_pairs={{0,4},{4,0},{8,12},{12,8},{16,20},{20,16},{24,28},{28,24},{1,5},{5... | collective-permute-start | bytes 196616 | tf_op jit(solution)/shard_map/ppermute | solution.py:10
  161.8 18.8 %collective-permute-start.5 = (bf16[32,2048]{1,0:T(8,128)(2,1)S(1)}, bf16[32,2048]{1,0:T(8,128)(2,1)S(1)}, u32[]{:S(2)}, u32[]{:S(2)}) collective-permute-start(bf16[32,2048]{1,0:T(8,128)(2,1)S(1)} %maximum_select_fusion.18), channel_id=1, source_target_pairs={{0,8},{4,12},{8,0},{12,4},{16,24},{20,28},{24,16},{28,20},{1,9},{5... | collective-permute-start | bytes 393224 | tf_op jit(solution)/shard_map/ppermute | solution.py:10
  167.5 4.1 %copy-start.11 = (s32[64,4]{0,1:T(4,128)S(1)}, s32[64,4]{0,1:T(4,128)}, u32[]{:S(2)}) copy-start(s32[64,4]{0,1:T(4,128)} %param.43) | copy-start | bytes 3076
  204.9 5.0 %collective-permute-start.6 = (bf16[32,512]{1,0:T(8,128)(2,1)S(1)}, bf16[32,512]{1,0:T(8,128)(2,1)S(1)}, u32[]{:S(2)}, u32[]{:S(2)}) collective-permute-start(bf16[32,512]{1,0:T(8,128)(2,1)S(1)} %select_convert_fusion), channel_id=1, source_target_pairs={{0,16},{4,20},{8,24},{12,28},{16,0},{20,4},{24,8},{28,12},{1,17},{... | collective-permute-start | bytes 98312 | tf_op jit(solution)/shard_map/ppermute | solution.py:10
  209.8 3.8 %collective-permute-start.7 = (bf16[32,256]{1,0:T(8,128)(2,1)S(1)}, bf16[32,256]{1,0:T(8,128)(2,1)S(1)}, u32[]{:S(2)}, u32[]{:S(2)}) collective-permute-start(bf16[32,256]{1,0:T(8,128)(2,1)S(1)} %select_convert_fusion.3), channel_id=1, source_target_pairs={{0,8},{4,12},{8,0},{12,4},{16,24},{20,28},{24,16},{28,20},{1,9},{5... | collective-permute-start | bytes 49160 | tf_op jit(solution)/shard_map/ppermute | solution.py:10
  211.3 71.6 %copy-start.4 = (bf16[4096,256]{0,1:T(8,128)(2,1)S(1)}, bf16[4096,256]{0,1:T(8,128)(2,1)}, u32[]{:S(2)}) copy-start(bf16[4096,256]{0,1:T(8,128)(2,1)} %get-tuple-element.10) | copy-start | bytes 6291460
  213.7 3.7 collective-permute-start.8
  222.6 3.9 %collective-permute-start.9 = (bf16[32,512]{1,0:T(8,128)(2,1)S(1)}, bf16[32,512]{1,0:T(8,128)(2,1)S(1)}, u32[]{:S(2)}, u32[]{:S(2)}) collective-permute-start(bf16[32,512]{1,0:T(8,128)(2,1)S(1)} %all_gather.36), channel_id=1, source_target_pairs={{0,4},{4,0},{8,12},{12,8},{16,20},{20,16},{24,28},{28,24},{1,5},{5... | collective-permute-start | bytes 98312 | tf_op jit(solution)/shard_map/ppermute | solution.py:10
  226.5 4.3 %collective-permute-start.10 = (bf16[32,1024]{1,0:T(8,128)(2,1)S(1)}, bf16[32,1024]{1,0:T(8,128)(2,1)S(1)}, u32[]{:S(2)}, u32[]{:S(2)}) collective-permute-start(bf16[32,1024]{1,0:T(8,128)(2,1)S(1)} %maximum_select_fusion.24), channel_id=1, source_target_pairs={{0,8},{4,12},{8,0},{12,4},{16,24},{20,28},{24,16},{28,20},{1,9},{5... | collective-permute-start | bytes 196616 | tf_op jit(solution)/shard_map/ppermute | solution.py:10
  230.9 67.5 %copy-start.6 = (bf16[4096,256]{1,0:T(8,128)(2,1)S(1)}, bf16[4096,256]{1,0:T(8,128)(2,1)}, u32[]{:S(2)}) copy-start(bf16[4096,256]{1,0:T(8,128)(2,1)} %param.33) | copy-start | bytes 6291460
  230.9 7.3 %collective-permute-start.11 = (bf16[32,2048]{1,0:T(8,128)(2,1)S(1)}, bf16[32,2048]{1,0:T(8,128)(2,1)S(1)}, u32[]{:S(2)}, u32[]{:S(2)}) collective-permute-start(bf16[32,2048]{1,0:T(8,128)(2,1)S(1)} %maximum_select_fusion.19), channel_id=1, source_target_pairs={{0,16},{4,20},{8,24},{12,28},{16,0},{20,4},{24,8},{28,12},{1,17},{... | collective-permute-start | bytes 393224 | tf_op jit(solution)/shard_map/ppermute | solution.py:10
  244.9 3.9 %collective-permute-start.12 = (bf16[32,512]{1,0:T(8,128)(2,1)S(1)}, bf16[32,512]{1,0:T(8,128)(2,1)S(1)}, u32[]{:S(2)}, u32[]{:S(2)}) collective-permute-start(bf16[32,512]{1,0:T(8,128)(2,1)S(1)} %all_gather.37), channel_id=1, source_target_pairs={{0,4},{4,0},{8,12},{12,8},{16,20},{20,16},{24,28},{28,24},{1,5},{5... | collective-permute-start | bytes 98312 | tf_op jit(solution)/shard_map/ppermute | solution.py:10
  248.8 4.3 %collective-permute-start.13 = (bf16[32,1024]{1,0:T(8,128)(2,1)S(1)}, bf16[32,1024]{1,0:T(8,128)(2,1)S(1)}, u32[]{:S(2)}, u32[]{:S(2)}) collective-permute-start(bf16[32,1024]{1,0:T(8,128)(2,1)S(1)} %maximum_select_fusion.25), channel_id=1, source_target_pairs={{0,8},{4,12},{8,0},{12,4},{16,24},{20,28},{24,16},{28,20},{1,9},{5... | collective-permute-start | bytes 196616 | tf_op jit(solution)/shard_map/ppermute | solution.py:10
  253.2 7.3 %collective-permute-start.14 = (bf16[32,2048]{1,0:T(8,128)(2,1)S(1)}, bf16[32,2048]{1,0:T(8,128)(2,1)S(1)}, u32[]{:S(2)}, u32[]{:S(2)}) collective-permute-start(bf16[32,2048]{1,0:T(8,128)(2,1)S(1)} %maximum_select_fusion.20), channel_id=1, source_target_pairs={{0,16},{4,20},{8,24},{12,28},{16,0},{20,4},{24,8},{28,12},{1,17},{... | collective-permute-start | bytes 393224 | tf_op jit(solution)/shard_map/ppermute | solution.py:10
  262.1 51.4 %copy-start.2 = (bf16[4096,512]{0,1:T(8,128)(2,1)S(1)}, bf16[4096,512]{0,1:T(8,128)(2,1)}, u32[]{:S(2)}) copy-start(bf16[4096,512]{0,1:T(8,128)(2,1)} %get-tuple-element.8) | copy-start | bytes 12582916
  267.4 3.9 %collective-permute-start.15 = (bf16[32,512]{1,0:T(8,128)(2,1)S(1)}, bf16[32,512]{1,0:T(8,128)(2,1)S(1)}, u32[]{:S(2)}, u32[]{:S(2)}) collective-permute-start(bf16[32,512]{1,0:T(8,128)(2,1)S(1)} %all_gather.38), channel_id=1, source_target_pairs={{0,4},{4,0},{8,12},{12,8},{16,20},{20,16},{24,28},{28,24},{1,5},{5... | collective-permute-start | bytes 98312 | tf_op jit(solution)/shard_map/ppermute | solution.py:10
  271.3 4.3 %collective-permute-start.16 = (bf16[32,1024]{1,0:T(8,128)(2,1)S(1)}, bf16[32,1024]{1,0:T(8,128)(2,1)S(1)}, u32[]{:S(2)}, u32[]{:S(2)}) collective-permute-start(bf16[32,1024]{1,0:T(8,128)(2,1)S(1)} %maximum_select_fusion.26), channel_id=1, source_target_pairs={{0,8},{4,12},{8,0},{12,4},{16,24},{20,28},{24,16},{28,20},{1,9},{5... | collective-permute-start | bytes 196616 | tf_op jit(solution)/shard_map/ppermute | solution.py:10
  275.7 7.3 %collective-permute-start.17 = (bf16[32,2048]{1,0:T(8,128)(2,1)S(1)}, bf16[32,2048]{1,0:T(8,128)(2,1)S(1)}, u32[]{:S(2)}, u32[]{:S(2)}) collective-permute-start(bf16[32,2048]{1,0:T(8,128)(2,1)S(1)} %maximum_select_fusion.21), channel_id=1, source_target_pairs={{0,16},{4,20},{8,24},{12,28},{16,0},{20,4},{24,8},{28,12},{1,17},{... | collective-permute-start | bytes 393224 | tf_op jit(solution)/shard_map/ppermute | solution.py:10
  289.0 4.3 %collective-permute-start.18 = (bf16[32,1024]{1,0:T(8,128)(2,1)S(1)}, bf16[32,1024]{1,0:T(8,128)(2,1)S(1)}, u32[]{:S(2)}, u32[]{:S(2)}) collective-permute-start(bf16[32,1024]{1,0:T(8,128)(2,1)S(1)} %all_gather.39), channel_id=1, source_target_pairs={{0,4},{4,0},{8,12},{12,8},{16,20},{20,16},{24,28},{28,24},{1,5},{5... | collective-permute-start | bytes 196616 | tf_op jit(solution)/shard_map/ppermute | solution.py:10
  293.3 32.8 %copy-start.5 = (bf16[4096,512]{1,0:T(8,128)(2,1)S(1)}, bf16[4096,512]{1,0:T(8,128)(2,1)}, u32[]{:S(2)}) copy-start(bf16[4096,512]{1,0:T(8,128)(2,1)} %param.32) | copy-start | bytes 12582916
  293.3 5.0 %collective-permute-start.19 = (bf16[32,2048]{1,0:T(8,128)(2,1)S(1)}, bf16[32,2048]{1,0:T(8,128)(2,1)S(1)}, u32[]{:S(2)}, u32[]{:S(2)}) collective-permute-start(bf16[32,2048]{1,0:T(8,128)(2,1)S(1)} %maximum_select_fusion.22), channel_id=1, source_target_pairs={{0,8},{4,12},{8,0},{12,4},{16,24},{20,28},{24,16},{28,20},{1,9},{5... | collective-permute-start | bytes 393224 | tf_op jit(solution)/shard_map/ppermute | solution.py:10
  304.0 4.3 %collective-permute-start.20 = (bf16[32,1024]{1,0:T(8,128)(2,1)S(1)}, bf16[32,1024]{1,0:T(8,128)(2,1)S(1)}, u32[]{:S(2)}, u32[]{:S(2)}) collective-permute-start(bf16[32,1024]{1,0:T(8,128)(2,1)S(1)} %all_gather.40), channel_id=1, source_target_pairs={{0,4},{4,0},{8,12},{12,8},{16,20},{20,16},{24,28},{28,24},{1,5},{5... | collective-permute-start | bytes 196616 | tf_op jit(solution)/shard_map/ppermute | solution.py:10
  308.4 5.0 %collective-permute-start.21 = (bf16[32,2048]{1,0:T(8,128)(2,1)S(1)}, bf16[32,2048]{1,0:T(8,128)(2,1)S(1)}, u32[]{:S(2)}, u32[]{:S(2)}) collective-permute-start(bf16[32,2048]{1,0:T(8,128)(2,1)S(1)} %maximum_select_fusion.23), channel_id=1, source_target_pairs={{0,8},{4,12},{8,0},{12,4},{16,24},{20,28},{24,16},{28,20},{1,9},{5... | collective-permute-start | bytes 393224 | tf_op jit(solution)/shard_map/ppermute | solution.py:10
  314.8 23.3 %copy-start.3 = (bf16[4096,384]{0,1:T(8,128)(2,1)S(1)}, bf16[4096,384]{0,1:T(8,128)(2,1)}, u32[]{:S(2)}) copy-start(bf16[4096,384]{0,1:T(8,128)(2,1)} %get-tuple-element.6) | copy-start | bytes 9437188
  320.4 24.3 %copy-start.7 = (bf16[1536,384]{1,0:T(8,128)(2,1)S(1)}, bf16[1536,384]{1,0:T(8,128)(2,1)}, u32[]{:S(2)}) copy-start(bf16[1536,384]{1,0:T(8,128)(2,1)} %param.28) | copy-start | bytes 3538948
  320.4 5.7 %collective-permute-start.22 = (bf16[32,2048]{1,0:T(8,128)(2,1)S(1)}, bf16[32,2048]{1,0:T(8,128)(2,1)S(1)}, u32[]{:S(2)}, u32[]{:S(2)}) collective-permute-start(bf16[32,2048]{1,0:T(8,128)(2,1)S(1)} %all_gather.41), channel_id=1, source_target_pairs={{0,4},{4,0},{8,12},{12,8},{16,20},{20,16},{24,28},{28,24},{1,5},{5... | collective-permute-start | bytes 393224 | tf_op jit(solution)/shard_map/ppermute | solution.py:10
  332.3 5.7 %collective-permute-start.23 = (bf16[32,2048]{1,0:T(8,128)(2,1)S(1)}, bf16[32,2048]{1,0:T(8,128)(2,1)S(1)}, u32[]{:S(2)}, u32[]{:S(2)}) collective-permute-start(bf16[32,2048]{1,0:T(8,128)(2,1)S(1)} %all_gather.42), channel_id=1, source_target_pairs={{0,4},{4,0},{8,12},{12,8},{16,20},{20,16},{24,28},{28,24},{1,5},{5... | collective-permute-start | bytes 393224 | tf_op jit(solution)/shard_map/ppermute | solution.py:10
Sparse Core Ops, SparseCore 0:
  57.8 21.2 reduce-scatter.3
  124.1 19.1 reduce-scatter.5
  184.8 19.1 reduce-scatter.7
where the time goes:
time: 380 us; the launch traced here: 378 us
  waiting for transfers between devices  133 us (35%)
  local copies, waits for them, and re-layouts  73.6 us (19%)
  blocking collectives  70.1 us (18%)
  starting transfers between devices  40.4 us (11%)
  other arithmetic  28.1 us (7%)
  matrix products  19.2 us (5%)
  between operations  13.6 us (4%)
    ppermute x24, waiting for transfers between devices, partner_2(): return lax.ppermute(value, axis, pairs)  73.6 us
    reduce_scatter x3, waiting for transfers between devices, per_device(): lax.psum_scatter(term.astype(jnp.bfloat16), 'front', scatter_dimension=1,...  59.3 us
    all_gather x9, blocking collectives, collect_group(): gathered = lax.all_gather(portion, 'front', axis=1, tiled=True)  48 us
    unnamed x36, local copies, waits for them, and re-layouts  34.5 us
    ppermute x24, starting transfers between devices, partner_2(): return lax.ppermute(value, axis, pairs)  33 us
    reshape x3, local copies, waits for them, and re-layouts, per_device(): shaped = link.reshape(group, fronts, piece, link.shape[1])  15.2 us
    mul x2, other arithmetic, per_device(): back = backs[level] * expanded[level]  11.9 us
    all_to_all x1, blocking collectives, per_device(): lax.all_to_all(outbound, ('leaf', 'front'), split_axis=1, concat_axis=1,...  11.2 us
  transfers between devices with their start and end apart: 28, of which 25 were waited for; matrix products, arithmetic and copies ran while one was open for 18% of the time, Pallas kernels for 0%

commit v1 on v0

--- a/solution.py
+++ b/solution.py
@@ -1,6 +1,10 @@
+import functools
+
 import jax
 import jax.numpy as jnp
 from jax import lax
+from jax.experimental import pallas as pl
+from jax.experimental.pallas import tpu as pltpu
 from jax.sharding import PartitionSpec as P
 
 
@@ -165,6 +169,457 @@
     return jnp.zeros_like(returned).at[:, send_order].set(returned)
 
 
+MESH = pl.DeviceIdType.MESH
+LANE = 128
+HALF = 64
+CORES = 2
+WEIGHTS = 14
+
+
+class Place:
+    def __init__(self, leaves, fronts):
+        self.leaves = leaves
+        self.fronts = fronts
+        self.across = fronts // CORES
+        self.leaf = lax.axis_index("leaf")
+        front = lax.axis_index("front")
+        self.front = front
+        self.x = front // CORES
+        self.core = front % CORES
+
+    def chips(self, group):
+        return group * self.across
+
+    def me(self, group):
+        return (self.leaf % group) * self.across + self.x
+
+    def device(self, group, chip):
+        base = self.leaf // group * group
+        return (base + chip // self.across, (chip % self.across) * CORES + self.core)
+
+    def sibling(self):
+        return (self.leaf, self.x * CORES + 1 - self.core)
+
+
+def drain(view, sem):
+    pltpu.make_async_copy(view, view, sem).wait()
+
+
+def chip_phase(place, group, source, slots, send_sem, recv_sem):
+    count = place.chips(group)
+    me = place.me(group)
+
+    def step(r, carry):
+        target = (me + count - r) % count
+        pltpu.make_async_remote_copy(
+            src_ref=source(target),
+            dst_ref=slots.at[r],
+            send_sem=send_sem,
+            recv_sem=recv_sem,
+            device_id=place.device(group, target),
+            device_id_type=MESH,
+        ).start()
+        return carry
+
+    lax.fori_loop(1, count, step, 0)
+
+
+def chip_wait(count, slots, send_sem, recv_sem):
+    view = slots.at[pl.ds(1, count - 1)]
+    drain(view, recv_sem)
+    drain(view, send_sem)
+
+
+def core_copy(place, source, target, send_sem, recv_sem):
+    copy = pltpu.make_async_remote_copy(
+        src_ref=source,
+        dst_ref=target,
+        send_sem=send_sem,
+        recv_sem=recv_sem,
+        device_id=place.sibling(),
+        device_id_type=MESH,
+    )
+    copy.start()
+    return copy
+
+
+def gather(place, group, value, slots, full, sems, beside=None):
+    count = place.chips(group)
+    me = place.me(group)
+    mine = slots.at[place.core]
+    width = value.shape[1]
+    mine[0] = value
+    chip_phase(place, group, lambda target: mine.at[0], mine, sems.at[0], sems.at[1])
+    if beside is not None:
+        beside()
+    chip_wait(count, mine, sems.at[0], sems.at[1])
+    copy = core_copy(place, mine, mine, sems.at[2], sems.at[3])
+    copy.wait()
+    for chip in range(count):
+        slot = (chip + count - me) % count
+        for core in range(CORES):
+            start = (chip * CORES + core) * width
+            full[:, start : start + width] = slots[core, slot]
+
+
+def product(full, weight, depth):
+    rows, cols = weight.shape
+    chunk = 512 if depth % 1024 else 1024
+
+    def step(index, total):
+        at = pl.ds(pl.multiple_of(index * chunk, chunk), chunk)
+        return total + jnp.dot(full[:, at], weight[at, :], preferred_element_type=jnp.float32)
+
+    return lax.fori_loop(0, depth // chunk, step, jnp.zeros((full.shape[0], cols), jnp.float32))
+
+
+def times_transposed(value, matrix):
+    return lax.dot_general(
+        value, matrix, (((1,), (1,)), ((), ())), preferred_element_type=jnp.float32
+    )
+
+
+def scatter_sum(place, group, value, link, terms, core_in, summed, chip_in, sems, beside=None):
+    count = place.chips(group)
+    me = place.me(group)
+    width = terms.shape[3]
+    chunk = 512
+    each = chunk // width
+
+    def step(index, carry):
+        at = pl.ds(pl.multiple_of(index * chunk, chunk), chunk)
+        part = times_transposed(value, link[at, :]).astype(jnp.bfloat16)
+        for inner in range(each):
+            piece = index * each + inner
+            terms[piece % CORES, piece // CORES] = part[:, inner * width : (inner + 1) * width]
+        return carry
+
+    lax.fori_loop(0, link.shape[0] // chunk, step, 0)
+    copy = core_copy(place, terms.at[1 - place.core], core_in, sems.at[0], sems.at[1])
+    copy.wait()
+    summed[...] = (
+        terms[place.core].astype(jnp.float32) + core_in[...].astype(jnp.float32)
+    ).astype(jnp.bfloat16)
+    chip_phase(
+        place, group, lambda target: summed.at[target], chip_in, sems.at[2], sems.at[3]
+    )
+    if beside is not None:
+        beside()
+    chip_wait(count, chip_in, sems.at[2], sems.at[3])
+    total = summed[me].astype(jnp.float32)
+    for slot in range(1, count):
+        total = total + chip_in[slot].astype(jnp.float32)
+    return total
+
+
+def exchange(place, parts, core_in, merged, chip_in, full, sems, first=None, second=None):
+    group = place.leaves
+    count = place.chips(group)
+    me = place.me(group)
+    copy = core_copy(place, parts, core_in, sems.at[0], sems.at[1])
+    if first is not None:
+        first()
+    copy.wait()
+    lanes = lax.broadcasted_iota(jnp.int32, (parts.shape[1], LANE), 1) // HALF
+    own = lanes == place.core
+
+    def merge(chip, carry):
+        other = pltpu.roll(core_in[chip].astype(jnp.float32), HALF, 1)
+        merged[chip] = jnp.where(own, parts[chip].astype(jnp.float32), other).astype(jnp.bfloat16)
+        return carry
+
+    lax.fori_loop(0, count, merge, 0)
+    chip_phase(
+        place, group, lambda target: merged.at[target], chip_in, sems.at[2], sems.at[3]
+    )
+    chip_in[0] = merged[me]
+    if second is not None:
+        second()
+    chip_wait(count, chip_in, sems.at[2], sems.at[3])
+    for chip in range(count):
+        full[:, chip * LANE : (chip + 1) * LANE] = chip_in[(chip + count - me) % count]
+
+
+def one_hot(index, rows):
+    spots = lax.broadcasted_iota(jnp.int32, (rows, index.shape[1]), 0)
+    return jnp.where(spots == index, 1.0, 0.0).astype(jnp.bfloat16)
+
+
+def solve_kernel(leaves, fronts, pieces, leaf_piece, *refs):
+    rhs, send_at, own_at, live, pattern = refs[:5]
+    sources = refs[5 : 5 + WEIGHTS]
+    out = refs[5 + WEIGHTS]
+    scratch = list(refs[6 + WEIGHTS :])
+
+    def take(number):
+        taken = scratch[:number]
+        del scratch[:number]
+        return taken
+
+    weights = take(WEIGHTS)
+    (weight_sem,) = take(1)
+    send_hot, own_hot = take(2)
+    ordered, full, wide = take(3)
+    out_trip = take(5)
+    back_trip = take(5)
+    leaf_down, leaf_down_sem, leaf_up, leaf_up_sem = take(4)
+    sums = [take(5) for _ in range(3)]
+    gathers = [take(2) for _ in range(9)]
+
+    place = Place(leaves, fronts)
+    count = place.chips(leaves)
+    me = place.me(leaves)
+    barrier = pltpu.get_barrier_semaphore()
+
+    def greet(r, carry):
+        target = (me + count - r) % count
+        pl.semaphore_signal(
+            barrier, inc=1, device_id=place.device(leaves, target), device_id_type=MESH
+        )
+        return carry
+
+    lax.fori_loop(1, count, greet, 0)
+    pl.semaphore_signal(barrier, inc=1, device_id=place.sibling(), device_id_type=MESH)
+    loads = [
+        pltpu.make_async_copy(sources[i], weights[i], weight_sem.at[i]) for i in range(WEIGHTS)
+    ]
+    for load in loads:
+        load.start()
+    (lower_leaf, down_1, lower_1, down_2, lower_2, down_3, lower_3) = weights[:7]
+    (upper_3, up_3, upper_2, up_2, upper_1, up_1, upper_leaf) = weights[7:]
+
+    def masked(index, offset):
+        def run():
+            loads[index].wait()
+            link = weights[index]
+            columns = link.shape[1]
+            block = link.shape[0] // pattern.shape[0]
+
+            def step(row, carry):
+                at = pl.ds(pl.multiple_of(row * block, block), block)
+                kept = pattern[row][:, offset : offset + columns].astype(jnp.bfloat16)
+                link[at, :] = link[at, :] * kept
+                return carry
+
+            lax.fori_loop(0, pattern.shape[0], step, 0)
+
+        return run
+
+    second_at = leaf_piece
+    third_at = leaf_piece + pieces[0]
+    starts = [0, leaves // 2, leaves // 2 + leaves // 4]
+    masks = []
+    for level in range(1, 4):
+        group = 2**level
+        piece = pieces[level - 1]
+        rows_live = live[starts[level - 1] + place.leaf // group]
+        first_row = ((place.leaf % group) * fronts + place.front) * piece
+        spots = lax.broadcasted_iota(jnp.int32, (1, piece), 1) + first_row
+        masks.append(jnp.where(spots < rows_live, 1.0, 0.0))
+
+    tile = 2 * LANE
+    parts, core_in, merged, chip_in, trip_sem = out_trip
+    rows_dev = rhs.shape[1]
+
+    def send_step(index, carry):
+        hot = one_hot(send_at[index], rows_dev)
+        send_hot[index] = hot
+        moved = jnp.dot(rhs[...], hot, preferred_element_type=jnp.float32).astype(jnp.bfloat16)
+        parts[2 * index] = moved[:, :LANE]
+        parts[2 * index + 1] = moved[:, LANE:]
+        return carry
+
+    lax.fori_loop(0, send_hot.shape[0], send_step, 0)
+    pl.semaphore_wait(barrier, count)
+
+    def owner_fill():
+        def step(index, carry):
+            own_hot[index] = one_hot(own_at[index], own_hot.shape[1])
+            return carry
+
+        lax.fori_loop(0, own_hot.shape[0], step, 0)
+
+    exchange(
+        place, parts, core_in, merged, chip_in, wide, trip_sem,
+        first=owner_fill, second=masked(1, 0),
+    )
+    for index in range(own_hot.shape[0]):
+        ordered[:, index * tile : (index + 1) * tile] = jnp.dot(
+            wide[...], own_hot[index], preferred_element_type=jnp.float32
+        ).astype(jnp.bfloat16)
+
+    gather(
+        place, 1, ordered[:, :leaf_piece], leaf_down, full, leaf_down_sem,
+        beside=masked(3, second_at),
+    )
+    loads[0].wait()
+    leaf_depth = leaf_piece * fronts
+    leaf_y = product(full, lower_leaf, leaf_depth).astype(jnp.bfloat16)
+
+    sep = lower_1.shape[0]
+    child = leaf_y
+    level_y = []
+    offset = leaf_piece
+    chores = [masked(5, third_at), masked(8, third_at), masked(10, second_at)]
+    late = [masked(12, 0), None, None]
+    for level in range(1, 4):
+        piece = pieces[level - 1]
+        total = scatter_sum(
+            place, 2**level, child, weights[2 * level - 1], *sums[level - 1],
+            beside=chores[level - 1],
+        )
+        own = ordered[:, offset : offset + piece].astype(jnp.float32)
+        offset = offset + piece
+        reduced = ((own - total) * masks[level - 1]).astype(jnp.bfloat16)
+        gather(place, 2**level, reduced, gathers[level - 1][0], full, gathers[level - 1][1],
+               beside=late[level - 1])
+        loads[2 * level].wait()
+        solved = product(full, weights[2 * level], sep)
+        child = (solved * masks[level - 1]).astype(jnp.bfloat16)
+        level_y.append(child)
+
+    gather(place, 8, level_y[2], gathers[3][0], full, gathers[3][1])
+    loads[7].wait()
+    found = (product(full, upper_3, sep) * masks[2]).astype(jnp.bfloat16)
+    starts_at = [leaf_piece, leaf_piece + pieces[0], leaf_piece + pieces[0] + pieces[1]]
+    ordered[:, starts_at[2] : starts_at[2] + pieces[2]] = found
+    turn = 4
+    for level, back, upper, load in ((2, up_3, upper_2, 9), (1, up_2, upper_1, 11)):
+        gather(place, 2 ** (level + 1), found, gathers[turn][0], full, gathers[turn][1])
+        update = level_y[level - 1].astype(jnp.float32) - product(full, back, sep)
+        reduced = (update * masks[level - 1]).astype(jnp.bfloat16)
+        gather(place, 2**level, reduced, gathers[turn + 1][0], full, gathers[turn + 1][1])
+        turn = turn + 2
+        loads[load].wait()
+        found = (product(full, upper, sep) * masks[level - 1]).astype(jnp.bfloat16)
+        ordered[:, starts_at[level - 1] : starts_at[level - 1] + pieces[level - 1]] = found
+    gather(place, 2, found, gathers[8][0], full, gathers[8][1])
+    update = (leaf_y.astype(jnp.float32) - product(full, up_1, sep)).astype(jnp.bfloat16)
+    gather(place, 1, update, leaf_up, full, leaf_up_sem)
+    loads[13].wait()
+    ordered[:, :leaf_piece] = product(full, upper_leaf, leaf_depth).astype(jnp.bfloat16)
+
+    parts, core_in, merged, chip_in, trip_sem = back_trip
+
+    def return_step(index, carry):
+        at = pl.ds(pl.multiple_of(index * tile, tile), tile)
+        moved = jnp.zeros((rhs.shape[0], tile), jnp.float32)
+        for inner in range(own_hot.shape[0]):
+            moved = moved + times_transposed(
+                ordered[:, inner * tile : (inner + 1) * tile], own_hot[inner, at, :]
+            )
+        moved = moved.astype(jnp.bfloat16)
+        parts[2 * index] = moved[:, :LANE]
+        parts[2 * index + 1] = moved[:, LANE:]
+        return carry
+
+    lax.fori_loop(0, count // 2, return_step, 0)
+    exchange(place, parts, core_in, merged, chip_in, wide, trip_sem)
+
+    for index in range(rows_dev // tile):
+        moved = jnp.zeros((rhs.shape[0], tile), jnp.float32)
+        for inner in range(send_hot.shape[0]):
+            moved = moved + times_transposed(
+                wide[:, inner * tile : (inner + 1) * tile],
+                send_hot[inner, index * tile : (index + 1) * tile, :],
+            )
+        out[:, index * tile : (index + 1) * tile] = moved.astype(jnp.bfloat16)
+
+
+def in_one_kernel(
+    leaves,
+    fronts,
+    right_side,
+    send_order,
+    owner_order,
+    live_rows,
+    lower_leaf,
+    upper_leaf,
+    lower_first,
+    lower_second,
+    lower_third,
+    upper_first,
+    upper_second,
+    upper_third,
+    downlink_first,
+    downlink_second,
+    downlink_third,
+    uplink_first,
+    uplink_second,
+    uplink_third,
+    pattern_first,
+    pattern_second,
+    pattern_third,
+):
+    columns, rows_dev = right_side.shape
+    devices = leaves * fronts
+    share = rows_dev // devices
+    chips = devices // CORES
+    sep = lower_first.shape[0]
+    block = sep // pattern_first.shape[0]
+    leaf_piece = lower_leaf.shape[1]
+    pieces = (lower_first.shape[1], lower_second.shape[1], lower_third.shape[1])
+    tile = 2 * LANE
+    send_at = jnp.pad(
+        send_order.reshape(devices, share), ((0, 0), (0, HALF - share)), constant_values=-1
+    ).reshape(-1, 1, tile)
+    own_at = (owner_order // share * HALF + owner_order % share).reshape(-1, 1, tile)
+    pattern = jnp.repeat(
+        jnp.concatenate([pattern_first, pattern_second, pattern_third], axis=1), block, axis=1
+    ).astype(jnp.float32)[:, None, :]
+    weights = [
+        lower_leaf, downlink_first, lower_first, downlink_second, lower_second, downlink_third,
+        lower_third, upper_third, uplink_third, upper_second, uplink_second, upper_first,
+        uplink_first, upper_leaf,
+    ]
+    half = jnp.bfloat16
+    dma = pltpu.SemaphoreType.DMA
+    scratch = [pltpu.VMEM(weight.shape, weight.dtype) for weight in weights]
+    scratch += [dma((WEIGHTS,))]
+    scratch += [
+        pltpu.VMEM((chips // 2, rows_dev, tile), half),
+        pltpu.VMEM((rows_dev // tile, chips * LANE, tile), half),
+        pltpu.VMEM((columns, rows_dev), half),
+        pltpu.VMEM((columns, sep), half),
+        pltpu.VMEM((columns, chips * LANE), half),
+    ]
+    for _ in range(2):
+        scratch += [pltpu.VMEM((chips, columns, LANE), half) for _ in range(4)] + [dma((4,))]
+    across = fronts // CORES
+    for _ in range(2):
+        scratch += [pltpu.VMEM((CORES, across, columns, leaf_piece), half), dma((4,))]
+    for level in range(1, 4):
+        slots = (2**level * across, columns, pieces[level - 1])
+        scratch += [pltpu.VMEM((CORES,) + slots, half)]
+        scratch += [pltpu.VMEM(slots, half) for _ in range(3)] + [dma((4,))]
+    for level in (1, 2, 3, 3, 3, 2, 2, 1, 1):
+        slots = (CORES, 2**level * across, columns, pieces[level - 1])
+        scratch += [pltpu.VMEM(slots, half), dma((4,))]
+    vmem = pl.BlockSpec(memory_space=pltpu.VMEM)
+    return pl.pallas_call(
+        functools.partial(solve_kernel, leaves, fronts, pieces, leaf_piece),
+        out_shape=jax.ShapeDtypeStruct((columns, rows_dev), half),
+        in_specs=[vmem, vmem, vmem, pl.BlockSpec(memory_space=pltpu.SMEM), vmem]
+        + [pl.BlockSpec(memory_space=pl.ANY)] * WEIGHTS,
+        out_specs=vmem,
+        scratch_shapes=scratch,
+        compiler_params=pltpu.CompilerParams(
+            collective_id=0, has_side_effects=True, vmem_limit_bytes=60 * 2**20
+        ),
+    )(right_side, send_at, own_at, live_rows, pattern, *weights)
+
+
+def choose(leaves, fronts, right_side, send_order, owner_order, live_rows, *matrices):
+    rows_dev = right_side.shape[1]
+    widths = [matrices[index].shape[1] for index in (0, 2, 3, 4)]
+    whole_lanes = all(width % LANE == 0 for width in widths)
+    if whole_lanes and rows_dev % (2 * LANE) == 0 and rows_dev // (leaves * fronts) <= HALF:
+        run = functools.partial(in_one_kernel, leaves, fronts)
+    else:
+        run = per_device
+    return run(right_side, send_order, owner_order, live_rows, *matrices)
+
+
 def solution(mesh):
     placed = (
         P(None, ("leaf", "front")),
@@ -190,7 +645,7 @@
         P(None, ("leaf", "front")),
     )
     return jax.shard_map(
-        per_device,
+        functools.partial(choose, mesh.shape["leaf"], mesh.shape["front"]),
         mesh=mesh,
         in_specs=placed,
         out_specs=P(None, ("leaf", "front")),

time: 380 us -> 127 us (0.33)
  waiting for transfers between devices: 133 us -> 0 us
  Pallas kernels: 0 us -> 120 us
  blocking collectives: 70.1 us -> 0 us
  local copies, waits for them, and re-layouts: 73.6 us -> 5.03 us
  starting transfers between devices: 40.4 us -> 0 us
  other arithmetic: 28.1 us -> 1.44 us
  matrix products: 19.2 us -> 0 us
  between operations: 13.6 us -> 0.03 us
    pallas_call x0 -> x1, Pallas kernels: none -> 120 us  [in_one_kernel(): pl.pallas_call(functools.partial(solve_kernel, leaves, fronts, pieces, le...]
    ppermute x24 -> x0, waiting for transfers between devices: 73.6 us -> none  [partner_2(): return lax.ppermute(value, axis, pairs)]
    reduce_scatter x3 -> x0, waiting for transfers between devices: 59.3 us -> none  [per_device(): lax.psum_scatter(term.astype(jnp.bfloat16), 'front', scatter_dimension=1,...]
    all_gather x11 -> x0, blocking collectives: 58.9 us -> none  [the longest x9 48 us: collect_group(): gathered = lax.all_gather(portion, 'front', axis=1, tiled=True)]
    ppermute x24 -> x0, starting transfers between devices: 33 us -> none  [partner_2(): return lax.ppermute(value, axis, pairs)]
    unnamed x36 -> x1, local copies, waits for them, and re-layouts: 34.5 us -> 1.53 us
    dot_general x14 -> x0, matrix products: 19.2 us -> none  [the longest x3 6.58 us: per_device(): jnp.einsum('kc,jfpc->kfjp', children, shaped, preferred_element_type=jnp....]
    mul x3 -> x0, other arithmetic: 17.8 us -> none  [the longest x2 11.9 us: per_device(): back = backs[level] * expanded[level]]
  transfers between devices with their start and end apart: 28 -> 0, of which waited for: 25 -> 0; matrix products, arithmetic and copies ran while one was open for 18% -> 0% of each run, Pallas kernels for 0% -> 0%
where the time goes in v1:
time: 127 us; the launch traced here: 126 us
  Pallas kernels  120 us (94%)
  local copies, waits for them, and re-layouts  5.03 us (4%)
  other arithmetic  1.44 us (1%)
    pallas_call x1, Pallas kernels, in_one_kernel(): pl.pallas_call(functools.partial(solve_kernel, leaves, fronts, pieces, le...  120 us

profile of v1, /device:TPU:0, one launch (start us, length us, event | category | flops | bytes accessed | tf_op | source)
XLA Modules:
  0.0 126.5 jit_solution(795912672806866728)
XLA Ops:
  0.0 0.7 add_convert_fusion
  0.7 0.1 copy.23
  0.8 0.3 broadcast_in_dim.4
  1.1 1.1 convert_element_type.16.refs_4_
  2.2 0.8 reshape.21
  3.0 0.7 reshape.22.refs_1_
  3.6 0.7 fusion.1
  4.4 0.6 reshape.23.refs_2_
  5.0 120.0 %shard_map.199 = bf16[32,1280]{1,0:T(8,128)(2,1)} custom-call(bf16[32,1280]{1,0:T(8,128)(2,1)} %refs_0_.1, s32[8,1,256]{2,1,0:T(1,128)} %reshape.22.refs_1_, s32[5,1,256]{2,1,0:T(1,128)} %reshape.23.refs_2_, s32[7]{0:T(128)} %refs_3_.1, f32[64,1,1152]{2,1,0:T(1,128)} %convert_element_type.16.refs_4_, bf16[1536,384]{1,0:T(8,128)(2,1)} %refs_5_.1, ...), custom_call_target="tpu_custom_call" | custom-call | tf_op jit(solution)/shard_map/pallas_call | solution.py:599
  125.0 1.5 %copy.26 = bf16[32,1280]{1,0:T(8,128)(2,1)} copy(bf16[32,1280]{1,0:T(8,128)(2,1)} %shard_map.199) | data formatting | bytes 163840
  (1 shorter events, 0.0 us)

commit v2 on v1

--- a/solution.py
+++ b/solution.py
@@ -243,34 +243,32 @@
     return copy
 
 
-def gather(place, group, value, slots, full, sems, beside=None):
+def half_product(slots, weight, core, me):
+    count = slots.shape[1]
+    pieces = [slots[core, (chip + count - me) % count] for chip in range(count)]
+    rows = weight[core]
+    return jnp.dot(
+        jnp.concatenate(pieces, axis=1),
+        rows.reshape(count * rows.shape[1], rows.shape[2]),
+        preferred_element_type=jnp.float32,
+    )
+
+
+def gather_product(place, group, value, slots, weight, sems, beside=None, load=None):
     count = place.chips(group)
     me = place.me(group)
     mine = slots.at[place.core]
-    width = value.shape[1]
     mine[0] = value
     chip_phase(place, group, lambda target: mine.at[0], mine, sems.at[0], sems.at[1])
     if beside is not None:
         beside()
     chip_wait(count, mine, sems.at[0], sems.at[1])
     copy = core_copy(place, mine, mine, sems.at[2], sems.at[3])
+    if load is not None:
+        load()
+    total = half_product(slots, weight, place.core, me)
     copy.wait()
-    for chip in range(count):
-        slot = (chip + count - me) % count
-        for core in range(CORES):
-            start = (chip * CORES + core) * width
-            full[:, start : start + width] = slots[core, slot]
-
-
-def product(full, weight, depth):
-    rows, cols = weight.shape
-    chunk = 512 if depth % 1024 else 1024
-
-    def step(index, total):
-        at = pl.ds(pl.multiple_of(index * chunk, chunk), chunk)
-        return total + jnp.dot(full[:, at], weight[at, :], preferred_element_type=jnp.float32)
-
-    return lax.fori_loop(0, depth // chunk, step, jnp.zeros((full.shape[0], cols), jnp.float32))
+    return total + half_product(slots, weight, 1 - place.core, me)
 
 
 def times_transposed(value, matrix):
@@ -283,19 +281,19 @@
     count = place.chips(group)
     me = place.me(group)
     width = terms.shape[3]
-    chunk = 512
-    each = chunk // width
-
-    def step(index, carry):
-        at = pl.ds(pl.multiple_of(index * chunk, chunk), chunk)
-        part = times_transposed(value, link[at, :]).astype(jnp.bfloat16)
-        for inner in range(each):
-            piece = index * each + inner
-            terms[piece % CORES, piece // CORES] = part[:, inner * width : (inner + 1) * width]
-        return carry
-
-    lax.fori_loop(0, link.shape[0] // chunk, step, 0)
+    each = 512 // width
+
+    def half(core):
+        for first in range(0, count, each):
+            rows = link[core, first : first + each]
+            part = times_transposed(value, rows.reshape(each * width, rows.shape[2]))
+            part = part.astype(jnp.bfloat16)
+            for inner in range(each):
+                terms[core, first + inner] = part[:, inner * width : (inner + 1) * width]
+
+    half(1 - place.core)
     copy = core_copy(place, terms.at[1 - place.core], core_in, sems.at[0], sems.at[1])
+    half(place.core)
     copy.wait()
     summed[...] = (
         terms[place.core].astype(jnp.float32) + core_in[...].astype(jnp.float32)
@@ -340,16 +338,24 @@
         full[:, chip * LANE : (chip + 1) * LANE] = chip_in[(chip + count - me) % count]
 
 
-def one_hot(index, rows):
-    spots = lax.broadcasted_iota(jnp.int32, (rows, index.shape[1]), 0)
-    return jnp.where(spots == index, 1.0, 0.0).astype(jnp.bfloat16)
+def fill_hot(target, index):
+    rows = 128
+
+    def step(block, carry):
+        first = pl.multiple_of(block * rows, rows)
+        spots = lax.broadcasted_iota(jnp.int32, (rows, index.shape[1]), 0) + first
+        target[pl.ds(first, rows), :] = jnp.where(spots == index, 1.0, 0.0).astype(jnp.bfloat16)
+        return carry
+
+    lax.fori_loop(0, target.shape[0] // rows, step, 0)
 
 
 def solve_kernel(leaves, fronts, pieces, leaf_piece, *refs):
-    rhs, send_at, own_at, live, pattern = refs[:5]
-    sources = refs[5 : 5 + WEIGHTS]
-    out = refs[5 + WEIGHTS]
-    scratch = list(refs[6 + WEIGHTS :])
+    rhs, send_at, own_at, live = refs[:4]
+    patterns = refs[4:7]
+    sources = refs[7 : 7 + WEIGHTS]
+    out = refs[7 + WEIGHTS]
+    scratch = list(refs[8 + WEIGHTS :])
 
     def take(number):
         taken = scratch[:number]
@@ -359,7 +365,7 @@
     weights = take(WEIGHTS)
     (weight_sem,) = take(1)
     send_hot, own_hot = take(2)
-    ordered, full, wide = take(3)
+    ordered, wide = take(2)
     out_trip = take(5)
     back_trip = take(5)
     leaf_down, leaf_down_sem, leaf_up, leaf_up_sem = take(4)
@@ -381,32 +387,54 @@
     lax.fori_loop(1, count, greet, 0)
     pl.semaphore_signal(barrier, inc=1, device_id=place.sibling(), device_id_type=MESH)
     loads = [
-        pltpu.make_async_copy(sources[i], weights[i], weight_sem.at[i]) for i in range(WEIGHTS)
+        [
+            pltpu.make_async_copy(
+                sources[i].at[:, core], weights[i].at[core], weight_sem.at[i, core]
+            )
+            for core in range(CORES)
+        ]
+        for i in range(WEIGHTS)
     ]
     for load in loads:
-        load.start()
+        for copy in load:
+            copy.start()
+
+    def ready(index):
+        for copy in loads[index]:
+            copy.wait()
+
     (lower_leaf, down_1, lower_1, down_2, lower_2, down_3, lower_3) = weights[:7]
     (upper_3, up_3, upper_2, up_2, upper_1, up_1, upper_leaf) = weights[7:]
 
-    def masked(index, offset):
+    def masked(index, pattern):
         def run():
-            loads[index].wait()
+            ready(index)
             link = weights[index]
-            columns = link.shape[1]
-            block = link.shape[0] // pattern.shape[0]
+            width, columns = link.shape[2:]
+            block = link.shape[1] * CORES * width // pattern.shape[0]
+            each = width // block
+            low = lax.broadcasted_iota(jnp.int32, (1, LANE), 1) < block
 
             def step(row, carry):
-                at = pl.ds(pl.multiple_of(row * block, block), block)
-                kept = pattern[row][:, offset : offset + columns].astype(jnp.bfloat16)
-                link[at, :] = link[at, :] * kept
+                kept = [
+                    jnp.where(
+                        low,
+                        pattern[row, 2 * pair].astype(jnp.float32),
+                        pattern[row, 2 * pair + 1].astype(jnp.float32),
+                    )
+                    for pair in range(columns // LANE)
+                ]
+                kept = jnp.concatenate(kept, axis=1).astype(jnp.bfloat16)
+                piece = row // each
+                at = pl.ds(pl.multiple_of(row % each * block, block), block)
+                spot = (piece % CORES, piece // CORES, at)
+                link[spot] = link[spot] * kept
                 return carry
 
             lax.fori_loop(0, pattern.shape[0], step, 0)
 
         return run
 
-    second_at = leaf_piece
-    third_at = leaf_piece + pieces[0]
     starts = [0, leaves // 2, leaves // 2 + leaves // 4]
     masks = []
     for level in range(1, 4):
@@ -422,9 +450,9 @@
     rows_dev = rhs.shape[1]
 
     def send_step(index, carry):
-        hot = one_hot(send_at[index], rows_dev)
-        send_hot[index] = hot
-        moved = jnp.dot(rhs[...], hot, preferred_element_type=jnp.float32).astype(jnp.bfloat16)
+        fill_hot(send_hot.at[index], send_at[index])
+        moved = jnp.dot(rhs[...], send_hot[index], preferred_element_type=jnp.float32)
+        moved = moved.astype(jnp.bfloat16)
         parts[2 * index] = moved[:, :LANE]
         parts[2 * index + 1] = moved[:, LANE:]
         return carry
@@ -434,34 +462,30 @@
 
     def owner_fill():
         def step(index, carry):
-            own_hot[index] = one_hot(own_at[index], own_hot.shape[1])
+            fill_hot(own_hot.at[index], own_at[index])
             return carry
 
         lax.fori_loop(0, own_hot.shape[0], step, 0)
 
     exchange(
         place, parts, core_in, merged, chip_in, wide, trip_sem,
-        first=owner_fill, second=masked(1, 0),
+        first=owner_fill, second=masked(1, patterns[0]),
     )
     for index in range(own_hot.shape[0]):
         ordered[:, index * tile : (index + 1) * tile] = jnp.dot(
             wide[...], own_hot[index], preferred_element_type=jnp.float32
         ).astype(jnp.bfloat16)
 
-    gather(
-        place, 1, ordered[:, :leaf_piece], leaf_down, full, leaf_down_sem,
-        beside=masked(3, second_at),
-    )
-    loads[0].wait()
-    leaf_depth = leaf_piece * fronts
-    leaf_y = product(full, lower_leaf, leaf_depth).astype(jnp.bfloat16)
-
-    sep = lower_1.shape[0]
+    leaf_y = gather_product(
+        place, 1, ordered[:, :leaf_piece], leaf_down, lower_leaf, leaf_down_sem,
+        beside=masked(3, patterns[1]), load=lambda: ready(0),
+    ).astype(jnp.bfloat16)
+
     child = leaf_y
     level_y = []
     offset = leaf_piece
-    chores = [masked(5, third_at), masked(8, third_at), masked(10, second_at)]
-    late = [masked(12, 0), None, None]
+    chores = [masked(5, patterns[2]), masked(8, patterns[2]), masked(10, patterns[1])]
+    late = [masked(12, patterns[0]), None, None]
     for level in range(1, 4):
         piece = pieces[level - 1]
         total = scatter_sum(
@@ -471,33 +495,41 @@
         own = ordered[:, offset : offset + piece].astype(jnp.float32)
         offset = offset + piece
         reduced = ((own - total) * masks[level - 1]).astype(jnp.bfloat16)
-        gather(place, 2**level, reduced, gathers[level - 1][0], full, gathers[level - 1][1],
-               beside=late[level - 1])
-        loads[2 * level].wait()
-        solved = product(full, weights[2 * level], sep)
+        solved = gather_product(
+            place, 2**level, reduced, gathers[level - 1][0], weights[2 * level],
+            gathers[level - 1][1], beside=late[level - 1],
+            load=functools.partial(ready, 2 * level),
+        )
         child = (solved * masks[level - 1]).astype(jnp.bfloat16)
         level_y.append(child)
 
-    gather(place, 8, level_y[2], gathers[3][0], full, gathers[3][1])
-    loads[7].wait()
-    found = (product(full, upper_3, sep) * masks[2]).astype(jnp.bfloat16)
+    found = gather_product(
+        place, 8, level_y[2], gathers[3][0], upper_3, gathers[3][1],
+        load=functools.partial(ready, 7),
+    )
+    found = (found * masks[2]).astype(jnp.bfloat16)
     starts_at = [leaf_piece, leaf_piece + pieces[0], leaf_piece + pieces[0] + pieces[1]]
     ordered[:, starts_at[2] : starts_at[2] + pieces[2]] = found
     turn = 4
     for level, back, upper, load in ((2, up_3, upper_2, 9), (1, up_2, upper_1, 11)):
-        gather(place, 2 ** (level + 1), found, gathers[turn][0], full, gathers[turn][1])
-        update = level_y[level - 1].astype(jnp.float32) - product(full, back, sep)
+        update = level_y[level - 1].astype(jnp.float32) - gather_product(
+            place, 2 ** (level + 1), found, gathers[turn][0], back, gathers[turn][1]
+        )
         reduced = (update * masks[level - 1]).astype(jnp.bfloat16)
-        gather(place, 2**level, reduced, gathers[turn + 1][0], full, gathers[turn + 1][1])
+        found = gather_product(
+            place, 2**level, reduced, gathers[turn + 1][0], upper, gathers[turn + 1][1],
+            load=functools.partial(ready, load),
+        )
         turn = turn + 2
-        loads[load].wait()
-        found = (product(full, upper, sep) * masks[level - 1]).astype(jnp.bfloat16)
+        found = (found * masks[level - 1]).astype(jnp.bfloat16)
         ordered[:, starts_at[level - 1] : starts_at[level - 1] + pieces[level - 1]] = found
-    gather(place, 2, found, gathers[8][0], full, gathers[8][1])
-    update = (leaf_y.astype(jnp.float32) - product(full, up_1, sep)).astype(jnp.bfloat16)
-    gather(place, 1, update, leaf_up, full, leaf_up_sem)
-    loads[13].wait()
-    ordered[:, :leaf_piece] = product(full, upper_leaf, leaf_depth).astype(jnp.bfloat16)
+    update = leaf_y.astype(jnp.float32) - gather_product(
+        place, 2, found, gathers[8][0], up_1, gathers[8][1]
+    )
+    ordered[:, :leaf_piece] = gather_product(
+        place, 1, update.astype(jnp.bfloat16), leaf_up, upper_leaf, leaf_up_sem,
+        load=functools.partial(ready, 13),
+    ).astype(jnp.bfloat16)
 
     parts, core_in, merged, chip_in, trip_sem = back_trip
 
@@ -555,8 +587,6 @@
     devices = leaves * fronts
     share = rows_dev // devices
     chips = devices // CORES
-    sep = lower_first.shape[0]
-    block = sep // pattern_first.shape[0]
     leaf_piece = lower_leaf.shape[1]
     pieces = (lower_first.shape[1], lower_second.shape[1], lower_third.shape[1])
     tile = 2 * LANE
@@ -564,23 +594,28 @@
         send_order.reshape(devices, share), ((0, 0), (0, HALF - share)), constant_values=-1
     ).reshape(-1, 1, tile)
     own_at = (owner_order // share * HALF + owner_order % share).reshape(-1, 1, tile)
-    pattern = jnp.repeat(
-        jnp.concatenate([pattern_first, pattern_second, pattern_third], axis=1), block, axis=1
-    ).astype(jnp.float32)[:, None, :]
     weights = [
         lower_leaf, downlink_first, lower_first, downlink_second, lower_second, downlink_third,
         lower_third, upper_third, uplink_third, upper_second, uplink_second, upper_first,
         uplink_first, upper_leaf,
     ]
+    levels = (0, 1, 1, 2, 2, 3, 3, 3, 3, 2, 2, 1, 1, 0)
+    weights = [
+        weight.reshape(
+            2**level * fronts // CORES, CORES, -1, weight.shape[1]
+        )
+        for weight, level in zip(weights, levels)
+    ]
     half = jnp.bfloat16
     dma = pltpu.SemaphoreType.DMA
-    scratch = [pltpu.VMEM(weight.shape, weight.dtype) for weight in weights]
-    scratch += [dma((WEIGHTS,))]
+    scratch = [
+        pltpu.VMEM((CORES, weight.shape[0]) + weight.shape[2:], weight.dtype) for weight in weights
+    ]
+    scratch += [dma((WEIGHTS, CORES))]
     scratch += [
         pltpu.VMEM((chips // 2, rows_dev, tile), half),
         pltpu.VMEM((rows_dev // tile, chips * LANE, tile), half),
         pltpu.VMEM((columns, rows_dev), half),
-        pltpu.VMEM((columns, sep), half),
         pltpu.VMEM((columns, chips * LANE), half),
     ]
     for _ in range(2):
@@ -599,20 +634,24 @@
     return pl.pallas_call(
         functools.partial(solve_kernel, leaves, fronts, pieces, leaf_piece),
         out_shape=jax.ShapeDtypeStruct((columns, rows_dev), half),
-        in_specs=[vmem, vmem, vmem, pl.BlockSpec(memory_space=pltpu.SMEM), vmem]
+        in_specs=[vmem, vmem, vmem]
+        + [pl.BlockSpec(memory_space=pltpu.SMEM)] * 4
         + [pl.BlockSpec(memory_space=pl.ANY)] * WEIGHTS,
         out_specs=vmem,
         scratch_shapes=scratch,
         compiler_params=pltpu.CompilerParams(
             collective_id=0, has_side_effects=True, vmem_limit_bytes=60 * 2**20
         ),
-    )(right_side, send_at, own_at, live_rows, pattern, *weights)
+    )(
+        right_side, send_at, own_at, live_rows, pattern_first, pattern_second, pattern_third, *weights
+    )
 
 
 def choose(leaves, fronts, right_side, send_order, owner_order, live_rows, *matrices):
     rows_dev = right_side.shape[1]
     widths = [matrices[index].shape[1] for index in (0, 2, 3, 4)]
     whole_lanes = all(width % LANE == 0 for width in widths)
+    whole_lanes = whole_lanes and matrices[6].shape[0] == HALF * matrices[14].shape[0]
     if whole_lanes and rows_dev % (2 * LANE) == 0 and rows_dev // (leaves * fronts) <= HALF:
         run = functools.partial(in_one_kernel, leaves, fronts)
     else:

time: 127 us -> 125 us (0.984)
  Pallas kernels: 120 us -> 116 us
  local copies, waits for them, and re-layouts: 5.03 us -> 7.73 us
    pallas_call x1, Pallas kernels: 120 us -> 116 us  [in_one_kernel(): pl.pallas_call(functools.partial(solve_kernel, leaves, fronts, pieces, le...]
    unnamed x1 -> x4, local copies, waits for them, and re-layouts: 1.53 us -> 5.67 us
where the time goes in v2:
time: 125 us; the launch traced here: 124 us
  Pallas kernels  116 us (93%)
  local copies, waits for them, and re-layouts  7.73 us (6%)
    pallas_call x1, Pallas kernels, in_one_kernel(): pl.pallas_call(functools.partial(solve_kernel, leaves, fronts, pieces, le...  116 us
    unnamed x4, local copies, waits for them, and re-layouts  5.67 us

profile of v2, /device:TPU:0, one launch (start us, length us, event | category | flops | bytes accessed | tf_op | source)
XLA Modules:
  0.0 124.2 jit_solution(11242896178152445288)
XLA Ops:
  0.0 0.7 fusion.1
  0.7 0.6 reshape.53.refs_2_
  1.3 0.8 reshape.51
  2.1 0.7 reshape.52.refs_1_
  2.8 1.4 %copy.22.refs_4_ = s32[64,6]{1,0:T(8,128)} copy(s32[64,6]{0,1:T(8,128)} %param.39) | data formatting | bytes 3072 | tf_op args[18]
  4.2 1.4 %copy.23.refs_5_ = s32[64,8]{1,0:T(8,128)} copy(s32[64,8]{0,1:T(8,128)} %param.40) | data formatting | bytes 4096 | tf_op args[19]
  5.5 1.4 %copy.24.refs_6_ = s32[64,4]{1,0:T(8,128)} copy(s32[64,4]{0,1:T(4,128)} %param.41) | data formatting | bytes 2048 | tf_op args[20]
  6.9 115.7 %shard_map.199 = bf16[32,1280]{1,0:T(8,128)(2,1)} custom-call(bf16[32,1280]{1,0:T(8,128)(2,1)} %refs_0_.1, s32[8,1,256]{2,1,0:T(1,128)} %reshape.52.refs_1_, s32[5,1,256]{2,1,0:T(1,128)} %reshape.53.refs_2_, s32[7]{0:T(128)} %refs_3_.1, s32[64,6]{1,0:T(8,128)} %copy.22.refs_4_, s32[64,8]{1,0:T(8,128)} %copy.23.refs_5_, s32[64,4]{1,0:T(8,128)} %copy.24.refs_6_, ...), custom_call_target="tpu_custom_call" | custom-call | tf_op jit(solution)/shard_map/pallas_call | solution.py:634
  122.7 1.5 %copy.26 = bf16[32,1280]{1,0:T(8,128)(2,1)} copy(bf16[32,1280]{1,0:T(8,128)(2,1)} %shard_map.199) | data formatting | bytes 163840
  (1 shorter events, 0.0 us)

commit v3 on v2

--- a/solution.py
+++ b/solution.py
@@ -184,18 +184,19 @@
         self.leaf = lax.axis_index("leaf")
         front = lax.axis_index("front")
         self.front = front
-        self.x = front // CORES
-        self.core = front % CORES
+        self.x = lax.div(front, CORES)
+        self.core = lax.rem(front, CORES)
 
     def chips(self, group):
         return group * self.across
 
     def me(self, group):
-        return (self.leaf % group) * self.across + self.x
+        return lax.rem(self.leaf, group) * self.across + self.x
 
     def device(self, group, chip):
-        base = self.leaf // group * group
-        return (base + chip // self.across, (chip % self.across) * CORES + self.core)
+        base = self.leaf - lax.rem(self.leaf, group)
+        inner = lax.div(chip, self.across)
+        return (base + inner, (chip - inner * self.across) * CORES + self.core)
 
     def sibling(self):
         return (self.leaf, self.x * CORES + 1 - self.core)
@@ -210,7 +211,7 @@
     me = place.me(group)
 
     def step(r, carry):
-        target = (me + count - r) % count
+        target = lax.rem(me + count - r, count)
         pltpu.make_async_remote_copy(
             src_ref=source(target),
             dst_ref=slots.at[r],
@@ -224,10 +225,8 @@
     lax.fori_loop(1, count, step, 0)
 
 
-def chip_wait(count, slots, send_sem, recv_sem):
-    view = slots.at[pl.ds(1, count - 1)]
-    drain(view, recv_sem)
-    drain(view, send_sem)
+def chip_wait(count, slots, sem):
+    drain(slots.at[pl.ds(1, count - 1)], sem)
 
 
 def core_copy(place, source, target, send_sem, recv_sem):
@@ -245,7 +244,7 @@
 
 def half_product(slots, weight, core, me):
     count = slots.shape[1]
-    pieces = [slots[core, (chip + count - me) % count] for chip in range(count)]
+    pieces = [slots[core, lax.rem(chip + count - me, count)] for chip in range(count)]
     rows = weight[core]
     return jnp.dot(
         jnp.concatenate(pieces, axis=1),
@@ -262,13 +261,16 @@
     chip_phase(place, group, lambda target: mine.at[0], mine, sems.at[0], sems.at[1])
     if beside is not None:
         beside()
-    chip_wait(count, mine, sems.at[0], sems.at[1])
+    chip_wait(count, mine, sems.at[1])
     copy = core_copy(place, mine, mine, sems.at[2], sems.at[3])
     if load is not None:
         load()
     total = half_product(slots, weight, place.core, me)
-    copy.wait()
-    return total + half_product(slots, weight, 1 - place.core, me)
+    copy.wait_recv()
+    total = total + half_product(slots, weight, 1 - place.core, me)
+    chip_wait(count, mine, sems.at[0])
+    copy.wait_send()
+    return total
 
 
 def times_transposed(value, matrix):
@@ -303,7 +305,8 @@
     )
     if beside is not None:
         beside()
-    chip_wait(count, chip_in, sems.at[2], sems.at[3])
+    chip_wait(count, chip_in, sems.at[3])
+    chip_wait(count, chip_in, sems.at[2])
     total = summed[me].astype(jnp.float32)
     for slot in range(1, count):
         total = total + chip_in[slot].astype(jnp.float32)
@@ -333,9 +336,10 @@
     chip_in[0] = merged[me]
     if second is not None:
         second()
-    chip_wait(count, chip_in, sems.at[2], sems.at[3])
+    chip_wait(count, chip_in, sems.at[3])
+    chip_wait(count, chip_in, sems.at[2])
     for chip in range(count):
-        full[:, chip * LANE : (chip + 1) * LANE] = chip_in[(chip + count - me) % count]
+        full[:, chip * LANE : (chip + 1) * LANE] = chip_in[lax.rem(chip + count - me, count)]
 
 
 def fill_hot(target, index):
@@ -378,7 +382,7 @@
     barrier = pltpu.get_barrier_semaphore()
 
     def greet(r, carry):
-        target = (me + count - r) % count
+        target = lax.rem(me + count - r, count)
         pl.semaphore_signal(
             barrier, inc=1, device_id=place.device(leaves, target), device_id_type=MESH
         )
@@ -406,12 +410,14 @@
     (lower_leaf, down_1, lower_1, down_2, lower_2, down_3, lower_3) = weights[:7]
     (upper_3, up_3, upper_2, up_2, upper_1, up_1, upper_leaf) = weights[7:]
 
-    def masked(index, pattern):
+    def masked(index, pattern, part=0, parts=1):
         def run():
-            ready(index)
+            if part == 0:
+                ready(index)
             link = weights[index]
             width, columns = link.shape[2:]
-            block = link.shape[1] * CORES * width // pattern.shape[0]
+            rows = pattern.shape[1]
+            block = link.shape[1] * CORES * width // rows
             each = width // block
             low = lax.broadcasted_iota(jnp.int32, (1, LANE), 1) < block
 
@@ -419,19 +425,19 @@
                 kept = [
                     jnp.where(
                         low,
-                        pattern[row, 2 * pair].astype(jnp.float32),
-                        pattern[row, 2 * pair + 1].astype(jnp.float32),
+                        pattern[2 * pair, row].astype(jnp.float32),
+                        pattern[2 * pair + 1, row].astype(jnp.float32),
                     )
                     for pair in range(columns // LANE)
                 ]
                 kept = jnp.concatenate(kept, axis=1).astype(jnp.bfloat16)
-                piece = row // each
-                at = pl.ds(pl.multiple_of(row % each * block, block), block)
-                spot = (piece % CORES, piece // CORES, at)
+                piece = lax.div(row, each)
+                at = pl.ds(pl.multiple_of((row - piece * each) * block, block), block)
+                spot = (lax.rem(piece, CORES), lax.div(piece, CORES), at)
                 link[spot] = link[spot] * kept
                 return carry
 
-            lax.fori_loop(0, pattern.shape[0], step, 0)
+            lax.fori_loop(rows * part // parts, rows * (part + 1) // parts, step, 0)
 
         return run
 
@@ -478,14 +484,16 @@
 
     leaf_y = gather_product(
         place, 1, ordered[:, :leaf_piece], leaf_down, lower_leaf, leaf_down_sem,
-        beside=masked(3, patterns[1]), load=lambda: ready(0),
+        beside=masked(3, patterns[1], 0, 2), load=lambda: ready(0),
     ).astype(jnp.bfloat16)
 
     child = leaf_y
     level_y = []
     offset = leaf_piece
-    chores = [masked(5, patterns[2]), masked(8, patterns[2]), masked(10, patterns[1])]
-    late = [masked(12, patterns[0]), None, None]
+    chores = [
+        masked(3, patterns[1], 1, 2), masked(5, patterns[2], 1, 2), masked(10, patterns[1], 0, 2)
+    ]
+    late = [masked(5, patterns[2], 0, 2), masked(8, patterns[2]), masked(10, patterns[1], 1, 2)]
     for level in range(1, 4):
         piece = pieces[level - 1]
         total = scatter_sum(
@@ -505,7 +513,7 @@
 
     found = gather_product(
         place, 8, level_y[2], gathers[3][0], upper_3, gathers[3][1],
-        load=functools.partial(ready, 7),
+        beside=masked(12, patterns[0], 0, 2), load=functools.partial(ready, 7),
     )
     found = (found * masks[2]).astype(jnp.bfloat16)
     starts_at = [leaf_piece, leaf_piece + pieces[0], leaf_piece + pieces[0] + pieces[1]]
@@ -513,7 +521,8 @@
     turn = 4
     for level, back, upper, load in ((2, up_3, upper_2, 9), (1, up_2, upper_1, 11)):
         update = level_y[level - 1].astype(jnp.float32) - gather_product(
-            place, 2 ** (level + 1), found, gathers[turn][0], back, gathers[turn][1]
+            place, 2 ** (level + 1), found, gathers[turn][0], back, gathers[turn][1],
+            beside=masked(12, patterns[0], 1, 2) if level == 2 else None,
         )
         reduced = (update * masks[level - 1]).astype(jnp.bfloat16)
         found = gather_product(
@@ -643,7 +652,8 @@
             collective_id=0, has_side_effects=True, vmem_limit_bytes=60 * 2**20
         ),
     )(
-        right_side, send_at, own_at, live_rows, pattern_first, pattern_second, pattern_third, *weights
+        right_side, send_at, own_at, live_rows, pattern_first.T, pattern_second.T,
+        pattern_third.T, *weights,
     )
 
 

time: 125 us -> 118 us (0.944)
  local copies, waits for them, and re-layouts: 7.73 us -> 3.59 us
  Pallas kernels: 116 us -> 113 us
    unnamed x4 -> x1, local copies, waits for them, and re-layouts: 5.67 us -> 1.53 us
    pallas_call x1, Pallas kernels: 116 us -> 113 us  [in_one_kernel(): pl.pallas_call(functools.partial(solve_kernel, leaves, fronts, pieces, le...]
where the time goes in v3:
time: 118 us; the launch traced here: 117 us
  Pallas kernels  113 us (96%)
  local copies, waits for them, and re-layouts  3.59 us (3%)
    pallas_call x1, Pallas kernels, in_one_kernel(): pl.pallas_call(functools.partial(solve_kernel, leaves, fronts, pieces, le...  113 us

profile of v3, /device:TPU:0, one launch (start us, length us, event | category | flops | bytes accessed | tf_op | source)
XLA Modules:
  0.0 117.3 jit_solution(4429884522250724752)
XLA Ops:
  0.0 0.7 fusion.1
  0.7 0.6 reshape.53.refs_2_
  1.3 0.8 reshape.51
  2.1 0.7 reshape.52.refs_1_
  2.8 113.0 %shard_map.199 = bf16[32,1280]{1,0:T(8,128)(2,1)} custom-call(bf16[32,1280]{1,0:T(8,128)(2,1)} %refs_0_.1, s32[8,1,256]{2,1,0:T(1,128)} %reshape.52.refs_1_, s32[5,1,256]{2,1,0:T(1,128)} %reshape.53.refs_2_, s32[7]{0:T(128)} %refs_3_.1, s32[6,64]{1,0:T(8,128)} %bitcast.31, s32[8,64]{1,0:T(8,128)} %bitcast.32, s32[4,64]{1,0:T(4,128)} %bitcast.33, ...), custom_call_target="tpu_custom_call" | custom-call | tf_op jit(solution)/shard_map/pallas_call | solution.py:643
  115.8 1.5 %copy.23 = bf16[32,1280]{1,0:T(8,128)(2,1)} copy(bf16[32,1280]{1,0:T(8,128)(2,1)} %shard_map.199) | data formatting | bytes 163840
  (1 shorter events, 0.0 us)
